TPU v7x, 512 devices: a whole 4x8x8 slice. The times are simulated.
512 devices in a mesh: lon: 32 (over z_lo, y, core), lat: 4 (over x), lev: 4 (over z_hi).
Axes of the slice: x: 4, y: 8, z: 8 (z_hi: 4, z_lo: 2; z = z_hi * 2 + z_lo), core: 2. Of those that a mesh axis runs over, the one named last changes fastest.
Arguments:
- bin_burden: float32 [9, 16, 32, 4096], P(None, 'lev', 'lat', 'lon'), may hold values from 0.05 to 5
- zonal_cfl_ratio: float32 [16, 32, 4096], P('lev', 'lat', 'lon'), may hold values from -0.24 to 0.24
- meridional_cfl_ratio: float32 [16, 32, 4096], P('lev', 'lat', 'lon'), may hold values from -0.24 to 0.24
- thermal_kelvins: float32 [16, 32, 4096], P('lev', 'lat', 'lon'), may hold values from 220 to 300
- diffusion_coefficient: float32 [16, 32, 4096], P('lev', 'lat', 'lon'), may hold values from 5 to 300
- inert_emitted_aerosol: float32 [16, 32, 4096], P('lev', 'lat', 'lon'), may hold values from 0.5 to 5
- heat_of_evaporation: float32 [9], replicated, may hold values from 50 to 150
- damped_parallels: int32 [8], replicated, may hold values from 0 to 31, as said below
- preserved_harmonic_limits: int32 [8], replicated, may hold values from 1 to 128, as said below
Outputs:
- condensed_mass: float32 [9, 16, 32, 4096], P(None, 'lev', 'lat', 'lon')
- gas_phase: float32 [9, 16, 32, 4096], P(None, 'lev', 'lat', 'lon')
Inputs may be any that keep to these rules, and one draw needn't show every extreme that they name: `damped_parallels`: entries 0 to 3 are distinct rows below 8, entry 0 being row 0; entries 4 to 7 are distinct rows of at least 24, entry 4 being row 31. preserved_harmonic_limits[0] = 1 and preserved_harmonic_limits[1] = 128.
All inputs are finite; a program needn't handle non-finite values.
Results may differ from a plain program's by a relative error of at most 0.0003.
Values sent between devices are 32-bit elements; how exact they have to be, the bound alone decides.
No kernel may reach another device: no remote copies, remote signals or barrier semaphores. Data moves between devices by JAX's collectives and lax.ppermute only.
A program may use at most 64 MiB of HBM per device.

v0:
```python
import math

import jax
import jax.numpy as jnp
import numpy as np
from jax import lax
from jax.experimental import pallas as pl
from jax.experimental.pallas import tpu as pltpu
from jax.sharding import PartitionSpec as P

BINS = 9
LEVELS = 4
TILES = BINS * LEVELS
ROWS = 8
WIDTH = 128
RING = 32
POLE = 4
CIRCLES = POLE * TILES
SHARE = 5
MODES = 128
CIRCLE = RING * WIDTH
PITERS = 3
GAS_CONST = 0.008314
REF_TEMP = 298.0
PRECISE = lax.Precision.HIGHEST
F32 = jnp.float32
VMEM = pl.BlockSpec(memory_space=pltpu.VMEM)
SMEM = pl.BlockSpec(memory_space=pltpu.SMEM)
GROUP = 40


def shape(*dims):
    return jax.ShapeDtypeStruct(dims, F32)


def call(kernel, name, outs, in_specs):
    return pl.pallas_call(
        kernel,
        out_shape=outs,
        in_specs=in_specs,
        out_specs=tuple(VMEM for _ in outs),
        compiler_params=pltpu.CompilerParams(vmem_limit_bytes=16 * 2**20),
        name=name,
    )


def tables():
    modes = np.arange(MODES)

    def pair(columns):
        angle = (columns[:, None] * modes[None, :] % CIRCLE) * (2.0 * math.pi / CIRCLE)
        return np.cos(angle), np.sin(angle)

    inner = np.stack(pair(np.arange(WIDTH))).astype(np.float32)
    first = pair(np.arange(RING) * WIDTH)
    before = pair(np.arange(RING) * WIDTH - 1)
    outer = np.stack([first[0], first[1], first[0] - before[0], first[1] - before[1]])
    return jnp.asarray(inner), jnp.asarray(outer.astype(np.float32))


def iotas():
    lane = lax.broadcasted_iota(jnp.int32, (ROWS, WIDTH), 1)
    row = lax.broadcasted_iota(jnp.int32, (ROWS, WIDTH), 0)
    return lane, row


def spread(row_vector):
    return jnp.broadcast_to(row_vector, (ROWS, WIDTH))


def column(tile, at):
    return jnp.broadcast_to(tile[:, at : at + 1], (ROWS, WIDTH))


def chosen_rows(rows_ref):
    southern = lax.axis_index("lat") >= 2
    return [
        jnp.clip(
            jnp.where(southern, rows_ref[POLE + p] - 3 * ROWS, rows_ref[p]), 0, ROWS - 1
        )
        for p in range(POLE)
    ]


def edge_kernel(burden, merid, out_a, out_b):
    even = lax.axis_index("lat") % 2 == 0
    row_a = jnp.where(even, ROWS - 1, 0)
    row_b = ROWS - 1 - row_a
    for t in range(TILES):
        out_a[t : t + 1, :] = burden[t, pl.ds(row_a, 1), :]
        out_b[t : t + 1, :] = burden[t, pl.ds(row_b, 1), :]
    for k in range(LEVELS):
        at = TILES + k
        out_a[at : at + 1, :] = merid[k, pl.ds(row_a, 1), :]
        out_b[at : at + 1, :] = merid[k, pl.ds(row_b, 1), :]


def squeeze_rows(tile, lane):
    packed = jnp.zeros_like(tile)
    for g in range(3):
        moved = pltpu.roll(tile, (5 - 3 * g) % ROWS, 0)
        if g:
            moved = pltpu.roll(moved, GROUP * g, 1)
        packed = jnp.where((lane >= GROUP * g) & (lane < GROUP * (g + 1)), moved, packed)
    return packed


def unsqueeze_rows(packed, row):
    tile = jnp.zeros_like(packed)
    for g in range(3):
        moved = pltpu.roll(packed, (3 * g - 5) % ROWS, 0)
        if g:
            moved = pltpu.roll(moved, WIDTH - GROUP * g, 1)
        tile = jnp.where((row >= 3 * g) & (row < 3 * g + 3), moved, tile)
    return tile


def advect_kernel(rows_ref, burden, zonal, merid, halo_a, halo_b, partial, sent, edges, packs):
    lane, row = iotas()
    lat = lax.axis_index("lat")
    even = lat % 2 == 0
    first_row = (row == 0) & (lat == 0)
    west_edge = jnp.zeros((ROWS, WIDTH), F32)
    east_edge = jnp.zeros((ROWS, WIDTH), F32)
    face_edge = jnp.zeros((ROWS, WIDTH), F32)
    for k in range(LEVELS):
        face = zonal[k]
        inner = jnp.where(lane == 0, 0.0, face)
        up, down = jnp.maximum(inner, 0.0), jnp.minimum(inner, 0.0)
        south = jnp.where(first_row, 0.0, merid[k])
        south_up, south_down = jnp.maximum(south, 0.0), jnp.minimum(south, 0.0)
        at = TILES + k
        north = spread(jnp.where(even, halo_a[at : at + 1, :], halo_b[at : at + 1, :]))
        north_up, north_down = jnp.maximum(north, 0.0), jnp.minimum(north, 0.0)
        face_edge = jnp.where((lane < TILES) & (lane % LEVELS == k), column(face, 0), face_edge)
        for b in range(BINS):
            t = b * LEVELS + k
            tile = burden[t]
            row_a, row_b = halo_a[t : t + 1, :], halo_b[t : t + 1, :]
            below, above = jnp.where(even, row_b, row_a), jnp.where(even, row_a, row_b)
            west = up * pltpu.roll(tile, 1, 1) + down * tile
            below_cells = jnp.where(row == 0, spread(below), pltpu.roll(tile, 1, 0))
            from_south = south_up * below_cells + south_down * tile
            to_north = jnp.where(
                row == ROWS - 1,
                north_up * tile + north_down * spread(above),
                pltpu.roll(from_south, ROWS - 1, 0),
            )
            partial[t] = (
                tile + west - pltpu.roll(west, WIDTH - 1, 1) + from_south - to_north
            )
            west_edge = jnp.where(lane == t, column(tile, 0), west_edge)
            east_edge = jnp.where(lane == t, column(tile, WIDTH - 1), east_edge)
    edges[0] = east_edge
    edges[1] = west_edge
    edges[2] = face_edge
    packs[0] = squeeze_rows(east_edge, lane)
    packs[1] = squeeze_rows(
        jnp.where(lane < TILES, west_edge, pltpu.roll(face_edge, TILES, 1)), lane
    )
    rows = chosen_rows(rows_ref)
    low = jnp.zeros((ROWS, WIDTH), F32)
    high = jnp.zeros((ROWS, WIDTH), F32)
    for p in range(POLE):
        picked = [edges[e, pl.ds(rows[p], 1), :] for e in range(3)]
        tile = jnp.where(row == 5, spread(picked[0]), jnp.where(row == 6, spread(picked[1]), spread(picked[2])))
        start = TILES * p
        moved = pltpu.roll(tile, start, 1) if start else tile
        low = jnp.where((lane >= start) & (lane < start + TILES), moved, low)
        if start + TILES > 100:
            moved = pltpu.roll(tile, (start - 100) % WIDTH, 1)
            high = jnp.where((lane >= start - 100) & (lane < start - 100 + TILES), moved, high)
    for j in range(RING):
        start = SHARE * j
        source, offset = (low, start) if start + SHARE <= WIDTH else (high, start - 100)
        moved = pltpu.roll(source, (WIDTH - offset) % WIDTH, 1) if offset else source
        sent[j, SHARE:, :] = moved[SHARE:]
        for i in range(SHARE):
            n = start + i
            if n < CIRCLES:
                sent[j, i : i + 1, :] = partial[n % TILES, pl.ds(rows[n // TILES], 1), :]
            else:
                sent[j, i : i + 1, :] = jnp.zeros((1, WIDTH), F32)


def filter_kernel(limits_ref, received, packs, inner, outer, returned, parts):
    lane, row = iotas()
    me = lax.axis_index("lon")
    southern = lax.axis_index("lat") >= 2
    block = received[...]
    cosine, sine = inner[0], inner[1]
    flat = block.reshape(RING * ROWS, WIDTH)
    parts[...] = jnp.dot(
        flat,
        jnp.concatenate([cosine, sine], axis=1),
        precision=PRECISE,
        preferred_element_type=F32,
    )
    cosine_part = jnp.zeros((ROWS, MODES), F32)
    sine_part = jnp.zeros((ROWS, MODES), F32)
    for q in range(RING):
        c, s = outer[0, q : q + 1, :], outer[1, q : q + 1, :]
        own_c = parts[ROWS * q : ROWS * (q + 1), :MODES]
        own_s = parts[ROWS * q : ROWS * (q + 1), MODES:]
        cosine_part += c * own_c - s * own_s
        sine_part += s * own_c + c * own_s
    east_cells = received[:, 5, :]
    west_cells = received[:, 6, :]
    faces = received[:, 7, :]
    beyond = pltpu.roll(east_cells, 1, 0)
    flux = jnp.maximum(faces, 0.0) * beyond + jnp.minimum(faces, 0.0) * west_cells
    flux_lane = lax.broadcasted_iota(jnp.int32, flux.shape, 1)
    flux = jnp.where(flux_lane < SHARE, flux, 0.0)
    edge = lax.dot_general(
        flux,
        jnp.concatenate([outer[2], outer[3]], axis=1),
        (((0,), (0,)), ((), ())),
        precision=PRECISE,
        preferred_element_type=F32,
    )
    cosine_part += edge[:ROWS, :MODES]
    sine_part += edge[:ROWS, MODES:]
    limit = jnp.zeros((ROWS, MODES), jnp.int32)
    for i in range(SHARE):
        p = jnp.minimum((me * SHARE + i) // TILES, POLE - 1)
        kept = limits_ref[p + jnp.where(southern, POLE, 0)]
        limit = jnp.where(row == i, kept, limit)
    weight = jnp.where(lane < limit, jnp.where(lane == 0, 1.0, 2.0), 0.0) * (1.0 / CIRCLE)
    cosine_part *= weight
    sine_part *= weight
    for q in range(RING):
        c, s = outer[0, q : q + 1, :], outer[1, q : q + 1, :]
        parts[ROWS * q : ROWS * (q + 1), :MODES] = cosine_part * c + sine_part * s
        parts[ROWS * q : ROWS * (q + 1), MODES:] = sine_part * c - cosine_part * s
    smooth = jnp.dot(
        parts[...],
        jnp.concatenate([cosine, sine], axis=0),
        precision=PRECISE,
        preferred_element_type=F32,
    )
    returned[...] = smooth.reshape(RING, ROWS, WIDTH)
    returned[(me + 1) % RING, SHARE:, :] = packs[0, SHARE:, :]
    returned[(me + RING - 1) % RING, SHARE:, :] = packs[1, SHARE:, :]


def column_kernel(rows_ref, partial, edges, back, diffusion, local, response, payload, filtered):
    lane, row = iotas()
    me = lax.axis_index("lon")
    lat = lax.axis_index("lat")
    east_own, west_own, face_own = edges[0], edges[1], edges[2]
    from_west = unsqueeze_rows(back[(me + RING - 1) % RING], row)
    from_east = unsqueeze_rows(back[(me + 1) % RING], row)
    four = jnp.where(lane < LEVELS, pltpu.roll(from_east, WIDTH - TILES, 1), 0.0)
    eight = four + pltpu.roll(four, 4, 1)
    sixteen = eight + pltpu.roll(eight, 8, 1)
    face_next = sixteen + pltpu.roll(sixteen, 16, 1) + pltpu.roll(four, 32, 1)
    flux_in = jnp.maximum(face_own, 0.0) * from_west + jnp.minimum(face_own, 0.0) * west_own
    flux_out = jnp.maximum(face_next, 0.0) * east_own + jnp.minimum(face_next, 0.0) * from_east
    for t in range(TILES):
        filtered[t] = (
            partial[t]
            + jnp.where(lane == 0, column(flux_in, t), 0.0)
            - jnp.where(lane == WIDTH - 1, column(flux_out, t), 0.0)
        )
    rows = chosen_rows(rows_ref)

    @pl.when((lat == 0) | (lat == 3))
    def _():
        for n in range(CIRCLES):
            filtered[n % TILES, pl.ds(rows[n // TILES], 1), :] = back[n // SHARE, n % SHARE : n % SHARE + 1, :]

    a1, a2, a3 = diffusion[1], diffusion[2], diffusion[3]
    i0 = 1.0 / (1.0 + a1)
    w1 = a1 * i0
    e1 = 1.0 + w1
    i1 = 1.0 / (e1 + a2)
    w2 = a2 * i1
    e2 = 1.0 + w2 * e1
    i2 = 1.0 / (e2 + a3)
    w3 = a3 * i2
    i3 = 1.0 / (1.0 + w3 * e2)
    up3 = i3
    up2 = w3 * up3
    up1 = w2 * up2
    up0 = w1 * up1
    d1 = w1
    d2 = w2 * d1
    d3 = w3 * d2
    low3 = d3 * i3
    low2 = d2 * i2 + w3 * low3
    low1 = d1 * i1 + w2 * low2
    low0 = i0 + w1 * low1
    for at, value in enumerate((low0, low1, low2, low3, up0, up1, up2, up3)):
        response[at] = value
    for b in range(BINS):
        f0 = filtered[b * LEVELS]
        f1 = filtered[b * LEVELS + 1] + w1 * f0
        f2 = filtered[b * LEVELS + 2] + w2 * f1
        f3 = filtered[b * LEVELS + 3] + w3 * f2
        x3 = f3 * i3
        x2 = f2 * i2 + w3 * x3
        x1 = f1 * i1 + w2 * x2
        x0 = f0 * i0 + w1 * x1
        local[b * LEVELS] = x0
        local[b * LEVELS + 1] = x1
        local[b * LEVELS + 2] = x2
        local[b * LEVELS + 3] = x3
        payload[b] = x0
        payload[BINS + b] = x3
    payload[2 * BINS] = low0
    payload[2 * BINS + 1] = up3
    payload[2 * BINS + 2] = up0
    payload[2 * BINS + 3] = 1.0 / diffusion[0]


def pair_kernel(own, other, payload, inside):
    lev = lax.axis_index("lev")
    lower = lev % 2 == 0
    bottom = lev < 2

    def of_lower(at):
        return jnp.where(lower, own[at], other[at])

    def of_upper(at):
        return jnp.where(lower, other[at], own[at])

    scale = 1.0 / (of_upper(2 * BINS + 3) + of_lower(2 * BINS + 1) + of_upper(2 * BINS))
    through = jnp.where(bottom, of_upper(2 * BINS + 2), of_lower(2 * BINS + 2))
    coupling = through * scale
    facing = jnp.where(bottom, of_upper(2 * BINS + 1), of_lower(2 * BINS))
    sign = jnp.where(bottom, 1.0, -1.0)
    signed = through * sign
    inside[BINS] = coupling
    payload[BINS] = facing - through * coupling
    payload[BINS + 1] = jnp.where(bottom, 0.0, of_lower(2 * BINS + 3))
    for b in range(BINS):
        flux = (of_lower(BINS + b) - of_upper(b)) * scale
        inside[b] = flux
        payload[b] = jnp.where(bottom, of_upper(BINS + b), of_lower(b)) + signed * flux


def phase_kernel(heat, own, other, inside, local, response, kelvins, inert, condensed, gas):
    lev = lax.axis_index("lev")
    lower = lev % 2 == 0
    middle = (lev == 1) | (lev == 2)
    sign = jnp.where(lev < 2, 1.0, -1.0)
    scale = sign / (own[BINS + 1] + other[BINS + 1] + own[BINS] + other[BINS])
    below, above = [], []
    for b in range(BINS):
        centre = (own[b] - other[b]) * scale
        mid = inside[b] + inside[BINS] * centre
        open_end = jnp.where(middle, centre, 0.0)
        below.append(jnp.where(lower, open_end, mid))
        above.append(jnp.where(lower, mid, open_end))
    for k in range(LEVELS):
        inverse = 1.0 / kelvins[k]
        ratio = REF_TEMP * inverse
        slope = (1.0 / REF_TEMP - inverse) * (1.0 / GAS_CONST)
        low, up = response[k], response[LEVELS + k]
        emitted = inert[k]
        totals, threshold = [], []
        for b in range(BINS):
            totals.append(local[b * LEVELS + k] + low * below[b] - up * above[b])
            threshold.append((10.0 ** (b - 2)) * ratio * jnp.exp(heat[b] * slope))
        organic = emitted
        for _ in range(PITERS):
            held = emitted
            for b in range(BINS):
                held = held + totals[b] * (organic / (organic + threshold[b]))
            organic = held
        for b in range(BINS):
            particle = totals[b] * (organic / (organic + threshold[b]))
            condensed[b * LEVELS + k] = particle
            gas[b * LEVELS + k] = totals[b] - particle


def body(
    bin_burden,
    zonal_cfl_ratio,
    meridional_cfl_ratio,
    thermal_kelvins,
    diffusion_coefficient,
    inert_emitted_aerosol,
    heat_of_evaporation,
    damped_parallels,
    preserved_harmonic_limits,
):
    burden = bin_burden.reshape(TILES, ROWS, WIDTH)
    inner, outer = tables()
    field = shape(TILES, ROWS, WIDTH)
    out_a, out_b = call(
        edge_kernel, "edge", (shape(GROUP, WIDTH), shape(GROUP, WIDTH)), [VMEM] * 2
    )(burden, meridional_cfl_ratio)
    halo_a = lax.ppermute(out_a, "lat", [(0, 1), (1, 0), (2, 3), (3, 2)])
    halo_b = lax.ppermute(out_b, "lat", [(1, 2), (2, 1)])
    partial, sent, edges, packs = call(
        advect_kernel,
        "advect",
        (field, shape(RING, ROWS, WIDTH), shape(3, ROWS, WIDTH), shape(2, ROWS, WIDTH)),
        [SMEM] + [VMEM] * 5,
    )(damped_parallels, burden, zonal_cfl_ratio, meridional_cfl_ratio, halo_a, halo_b)
    received = lax.all_to_all(sent, "lon", 0, 0, tiled=True)
    returned, _ = call(
        filter_kernel,
        "filter",
        (shape(RING, ROWS, WIDTH), shape(RING * ROWS, 2 * MODES)),
        [SMEM] + [VMEM] * 4,
    )(preserved_harmonic_limits, received, packs, inner, outer)
    back = lax.all_to_all(returned, "lon", 0, 0, tiled=True)
    ends = shape(2 * BINS + 4, ROWS, WIDTH)
    local, response, payload, _ = call(
        column_kernel,
        "column",
        (field, shape(2 * LEVELS, ROWS, WIDTH), ends, field),
        [SMEM] + [VMEM] * 4,
    )(damped_parallels, partial, edges, back, diffusion_coefficient)
    partner = lax.ppermute(payload, "lev", [(0, 1), (1, 0), (2, 3), (3, 2)])
    facing, inside = call(
        pair_kernel,
        "pair",
        (shape(BINS + 2, ROWS, WIDTH), shape(BINS + 1, ROWS, WIDTH)),
        [VMEM] * 2,
    )(payload, partner)
    across = lax.ppermute(facing, "lev", [(0, 3), (3, 0), (1, 2), (2, 1)])
    condensed, gas = call(phase_kernel, "phase", (field, field), [SMEM] + [VMEM] * 7)(
        heat_of_evaporation,
        facing,
        across,
        inside,
        local,
        response,
        thermal_kelvins,
        inert_emitted_aerosol,
    )
    return condensed.reshape(bin_burden.shape), gas.reshape(bin_burden.shape)


def solution(mesh):
    block = P("lev", "lat", "lon")
    binned = P(None, "lev", "lat", "lon")
    return jax.shard_map(
        body,
        mesh=mesh,
        in_specs=(binned, block, block, block, block, block, P(), P(), P()),
        out_specs=(binned, binned),
        check_vma=False,
    )
```

profile of v0, /device:TPU:4, one launch (start us, length us, event | category | flops | bytes accessed | tf_op | source)
XLA Modules:
  0.0 71.4 jit_solution(17479435050758394157)
XLA Ops:
  0.6 0.0 copy-start
  0.6 0.9 %copy-done = f32[9,4,8,128]{3,2,1,0:T(8,128)S(1)} copy-done((f32[9,4,8,128]{3,2,1,0:T(8,128)S(1)}, f32[9,4,8,128]{3,2,1,0:T(8,128)}, u32[]{:S(2)}) %copy-start) | copy-done | bytes 147480
  1.5 0.0 copy-start.2
  1.5 0.7 %copy-done.2 = f32[4,8,128]{2,1,0:T(8,128)S(1)} copy-done((f32[4,8,128]{2,1,0:T(8,128)S(1)}, f32[4,8,128]{2,1,0:T(8,128)}, u32[]{:S(2)}) %copy-start.2) | copy-done | bytes 16408
  2.3 0.0 copy-start.4
  2.3 0.0 copy-start.8
  2.3 3.1 %collective-permute-start = (f32[40,128]{1,0:T(8,128)S(1)}, f32[40,128]{1,0:T(8,128)S(1)}, u32[]{:S(2)}, u32[]{:S(2)}) collective-permute-start(f32[40,128]{1,0:T(8,128)S(1)} %get-tuple-element.16), channel_id=1, source_target_pairs={{0,4},{4,0},{8,12},{12,8},{1,5},{5,1},{9,13},{13,9},{2,6},{6,2},{1... | collective-permute-start | bytes 61448 | tf_op jit(solution)/shard_map/ppermute | solution.py:394
  5.4 7.2 %collective-permute-start.1 = (f32[40,128]{1,0:T(8,128)S(1)}, f32[40,128]{1,0:T(8,128)S(1)}, u32[]{:S(2)}, u32[]{:S(2)}) collective-permute-start(f32[40,128]{1,0:T(8,128)S(1)} %get-tuple-element.17), channel_id=1, source_target_pairs={{4,8},{8,4},{5,9},{9,5},{6,10},{10,6},{7,11},{11,7},{20,24},{24,20... | collective-permute-start | bytes 61448 | tf_op jit(solution)/shard_map/ppermute | solution.py:395
  12.6 0.0 collective-permute-done.halo_a
  12.6 1.7 %collective-permute-done.1.halo_b = f32[40,128]{1,0:T(8,128)S(1)} collective-permute-done((f32[40,128]{1,0:T(8,128)S(1)}, f32[40,128]{1,0:T(8,128)S(1)}, u32[]{:S(2)}, u32[]{:S(2)}) %collective-permute-start.1) | collective-permute-done | bytes 20512 | tf_op jit(solution)/shard_map/ppermute | solution.py:395
  14.3 0.0 copy-done.4
  14.3 0.0 copy-done.8
  14.3 1.3 %advect.1 = (f32[36,8,128]{2,1,0:T(8,128)S(1)}, f32[32,8,128]{2,1,0:T(8,128)S(1)}, f32[3,8,128]{2,1,0:T(8,128)S(1)}, f32[2,8,128]{2,1,0:T(8,128)S(1)}) custom-call(s32[8]{0:T(128)S(1)} %copy-done.8, f32[36,8,128]{2,1,0:T(8,128)S(1)} %bitcast.4, f32[4,8,128]{2,1,0:T(8,128)S(1)} %copy-done.4, f32[4,8,128]{2,1,0:T(8,128)S(1)} %copy-done.2, ...), custom_call_target="tpu_custom_call" | custom-call | tf_op jit(solution)/shard_map/advect/pallas_call | solution.py:396
  15.7 0.0 copy-start.1
  15.7 0.0 copy-start.3
  15.7 16.5 %all_to_all.10.received = f32[32,8,128]{2,1,0:T(8,128)S(1)} all-to-all(f32[32,8,128]{2,1,0:T(8,128)S(1)} %get-tuple-element.20), channel_id=1, replica_groups=mesh['lon'=32,'lat'=4,'lev'=4] {'lon'}, dimensions={0} | all-to-all | bytes 262144 | tf_op jit(solution)/shard_map/all_to_all | solution.py:402
  32.1 0.0 copy-start.9
  32.1 0.0 copy-done.1
  32.1 0.0 copy-done.3
  32.1 0.6 copy-done.9
  32.8 1.9 %filter.1 = (f32[32,8,128]{2,1,0:T(8,128)S(1)}, f32[256,256]{1,0:T(8,128)}) custom-call(s32[8]{0:T(128)S(1)} %copy-done.9, f32[32,8,128]{2,1,0:T(8,128)S(1)} %all_to_all.10.received, f32[2,8,128]{2,1,0:T(8,128)S(1)} %get-tuple-element.21.packs, f32[2,128,128]{2,1,0:T(8,128)S(1)} %copy-done.1, f32[4,32,128]{2,1,0:T(8,128)S(1)} %copy-done.3), custom_call_target="tpu_custom_call" | custom-call | tf_op jit(solution)/shard_map/filter/pallas_call | solution.py:403
  34.7 0.0 copy-start.5
  34.7 13.5 %all_to_all.11.back = f32[32,8,128]{2,1,0:T(8,128)S(1)} all-to-all(f32[32,8,128]{2,1,0:T(8,128)S(1)} %get-tuple-element.22), channel_id=1, replica_groups=mesh['lon'=32,'lat'=4,'lev'=4] {'lon'}, dimensions={0} | all-to-all | bytes 262144 | tf_op jit(solution)/shard_map/all_to_all | solution.py:409
  48.2 0.0 copy-done.5
  48.2 1.7 %column.1 = (f32[36,8,128]{2,1,0:T(8,128)S(1)}, f32[8,8,128]{2,1,0:T(8,128)S(1)}, f32[22,8,128]{2,1,0:T(8,128)S(1)}, f32[36,8,128]{2,1,0:T(8,128)}) custom-call(s32[8]{0:T(128)S(1)} %copy-done.8, f32[36,8,128]{2,1,0:T(8,128)S(1)} %get-tuple-element.18.partial, f32[3,8,128]{2,1,0:T(8,128)S(1)} %get-tuple-element.19.edges, f32[32,8,128]{2,1,0:T(8,128)S(1)} %all_to_all.11.back, ...), custom_call_target="tpu_custom_call" | custom-call | tf_op jit(solution)/shard_map/column/pallas_call | solution.py:411
  49.9 6.1 %collective-permute-start.2 = (f32[22,8,128]{2,1,0:T(8,128)S(1)}, f32[22,8,128]{2,1,0:T(8,128)S(1)}, u32[]{:S(2)}, u32[]{:S(2)}) collective-permute-start(f32[22,8,128]{2,1,0:T(8,128)S(1)} %get-tuple-element.23.own), channel_id=1, source_target_pairs={{0,1},{1,0},{2,3},{3,2},{4,5},{5,4},{6,7},{7,6},{8,9},{9,8},{10,11... | collective-permute-start | bytes 270344 | tf_op jit(solution)/shard_map/ppermute | solution.py:417
  56.0 3.5 %collective-permute-done.2.other = f32[22,8,128]{2,1,0:T(8,128)S(1)} collective-permute-done((f32[22,8,128]{2,1,0:T(8,128)S(1)}, f32[22,8,128]{2,1,0:T(8,128)S(1)}, u32[]{:S(2)}, u32[]{:S(2)}) %collective-permute-start.2) | collective-permute-done | bytes 90144 | tf_op jit(solution)/shard_map/ppermute | solution.py:417
  59.5 0.0 copy-start.6
  59.5 0.0 copy-start.7
  59.5 7.8 %collective-permute-start.3 = (f32[11,8,128]{2,1,0:T(8,128)S(1)}, f32[11,8,128]{2,1,0:T(8,128)S(1)}, u32[]{:S(2)}, u32[]{:S(2)}) collective-permute-start(f32[11,8,128]{2,1,0:T(8,128)S(1)} %get-tuple-element.24.own), channel_id=1, source_target_pairs={{0,3},{3,0},{1,2},{2,1},{4,7},{7,4},{5,6},{6,5},{8,11},{11,8},{9,1... | collective-permute-start | bytes 135176 | tf_op jit(solution)/shard_map/ppermute | solution.py:424
  67.3 2.0 %collective-permute-done.3.other = f32[11,8,128]{2,1,0:T(8,128)S(1)} collective-permute-done((f32[11,8,128]{2,1,0:T(8,128)S(1)}, f32[11,8,128]{2,1,0:T(8,128)S(1)}, u32[]{:S(2)}, u32[]{:S(2)}) %collective-permute-start.3) | collective-permute-done | bytes 45088 | tf_op jit(solution)/shard_map/ppermute | solution.py:424
  69.3 0.0 copy-start.10
  69.3 0.0 copy-done.6
  69.3 0.0 copy-done.7
  69.3 0.6 copy-done.10
  70.0 1.5 %phase.1 = (f32[36,8,128]{2,1,0:T(8,128)}, f32[36,8,128]{2,1,0:T(8,128)}) custom-call(f32[9]{0:T(128)S(1)} %copy-done.10, f32[11,8,128]{2,1,0:T(8,128)S(1)} %get-tuple-element.24.own, f32[11,8,128]{2,1,0:T(8,128)S(1)} %collective-permute-done.3.other, f32[10,8,128]{2,1,0:T(8,128)S(1)} %get-tuple-element.25.inside, ...), custom_call_target="tpu_custom_call" | custom-call | tf_op jit(solution)/shard_map/phase/pallas_call | solution.py:425
  (2 shorter events, 0.1 us)
Async XLA Ops:
  0.6 0.9 %copy-start = (f32[9,4,8,128]{3,2,1,0:T(8,128)S(1)}, f32[9,4,8,128]{3,2,1,0:T(8,128)}, u32[]{:S(2)}) copy-start(f32[9,4,8,128]{3,2,1,0:T(8,128)} %param.11) | copy-start | bytes 442372
  1.5 0.7 %copy-start.2 = (f32[4,8,128]{2,1,0:T(8,128)S(1)}, f32[4,8,128]{2,1,0:T(8,128)}, u32[]{:S(2)}) copy-start(f32[4,8,128]{2,1,0:T(8,128)} %merid.3) | copy-start | bytes 49156
  2.3 12.1 %copy-start.4 = (f32[4,8,128]{2,1,0:T(8,128)S(1)}, f32[4,8,128]{2,1,0:T(8,128)}, u32[]{:S(2)}) copy-start(f32[4,8,128]{2,1,0:T(8,128)} %zonal.1) | copy-start | bytes 49156
  2.3 12.0 %copy-start.8 = (s32[8]{0:T(128)S(1)}, s32[8]{0:T(128)}, u32[]{:S(2)}) copy-start(s32[8]{0:T(128)} %rows_ref.3) | copy-start | bytes 100
  2.3 10.3 %collective-permute-start = (f32[40,128]{1,0:T(8,128)S(1)}, f32[40,128]{1,0:T(8,128)S(1)}, u32[]{:S(2)}, u32[]{:S(2)}) collective-permute-start(f32[40,128]{1,0:T(8,128)S(1)} %get-tuple-element.16), channel_id=1, source_target_pairs={{0,4},{4,0},{8,12},{12,8},{1,5},{5,1},{9,13},{13,9},{2,6},{6,2},{1... | collective-permute-start | bytes 61448 | tf_op jit(solution)/shard_map/ppermute | solution.py:394
  5.4 8.9 %collective-permute-start.1 = (f32[40,128]{1,0:T(8,128)S(1)}, f32[40,128]{1,0:T(8,128)S(1)}, u32[]{:S(2)}, u32[]{:S(2)}) collective-permute-start(f32[40,128]{1,0:T(8,128)S(1)} %get-tuple-element.17), channel_id=1, source_target_pairs={{4,8},{8,4},{5,9},{9,5},{6,10},{10,6},{7,11},{11,7},{20,24},{24,20... | collective-permute-start | bytes 61448 | tf_op jit(solution)/shard_map/ppermute | solution.py:395
  15.7 16.5 %copy-start.1 = (f32[2,128,128]{2,1,0:T(8,128)S(1)}, f32[2,128,128]{2,1,0:T(8,128)}, u32[]{:S(2)}) copy-start(f32[2,128,128]{2,1,0:T(8,128)} %constant.4.clone.inner) | copy-start | bytes 393220
  15.7 16.5 %copy-start.3 = (f32[4,32,128]{2,1,0:T(8,128)S(1)}, f32[4,32,128]{2,1,0:T(8,128)}, u32[]{:S(2)}) copy-start(f32[4,32,128]{2,1,0:T(8,128)} %constant.5.clone.outer) | copy-start | bytes 196612
  32.1 0.7 copy-start.9
  34.7 13.5 %copy-start.5 = (f32[4,8,128]{2,1,0:T(8,128)S(1)}, f32[4,8,128]{2,1,0:T(8,128)}, u32[]{:S(2)}) copy-start(f32[4,8,128]{2,1,0:T(8,128)} %diffusion.1) | copy-start | bytes 49156
  49.9 9.6 %collective-permute-start.2 = (f32[22,8,128]{2,1,0:T(8,128)S(1)}, f32[22,8,128]{2,1,0:T(8,128)S(1)}, u32[]{:S(2)}, u32[]{:S(2)}) collective-permute-start(f32[22,8,128]{2,1,0:T(8,128)S(1)} %get-tuple-element.23.own), channel_id=1, source_target_pairs={{0,1},{1,0},{2,3},{3,2},{4,5},{5,4},{6,7},{7,6},{8,9},{9,8},{10,11... | collective-permute-start | bytes 270344 | tf_op jit(solution)/shard_map/ppermute | solution.py:417
  59.5 9.8 %copy-start.6 = (f32[4,8,128]{2,1,0:T(8,128)S(1)}, f32[4,8,128]{2,1,0:T(8,128)}, u32[]{:S(2)}) copy-start(f32[4,8,128]{2,1,0:T(8,128)} %kelvins.1) | copy-start | bytes 49156
  59.5 9.8 %copy-start.7 = (f32[4,8,128]{2,1,0:T(8,128)S(1)}, f32[4,8,128]{2,1,0:T(8,128)}, u32[]{:S(2)}) copy-start(f32[4,8,128]{2,1,0:T(8,128)} %inert.1) | copy-start | bytes 49156
  59.5 9.8 %collective-permute-start.3 = (f32[11,8,128]{2,1,0:T(8,128)S(1)}, f32[11,8,128]{2,1,0:T(8,128)S(1)}, u32[]{:S(2)}, u32[]{:S(2)}) collective-permute-start(f32[11,8,128]{2,1,0:T(8,128)S(1)} %get-tuple-element.24.own), channel_id=1, source_target_pairs={{0,3},{3,0},{1,2},{2,1},{4,7},{7,4},{5,6},{6,5},{8,11},{11,8},{9,1... | collective-permute-start | bytes 135176 | tf_op jit(solution)/shard_map/ppermute | solution.py:424
  69.3 0.7 copy-start.10
where the time goes:
time: 71.9 us; the launch traced here: 71.4 us
  blocking collectives  30 us (42%)
  starting transfers between devices  24.1 us (34%)
  waiting for transfers between devices  7.25 us (10%)
  Pallas kernels  6.4 us (9%)
  local copies, waits for them, and re-layouts  2.95 us (4%)
  between operations  0.73 us (1%)
    all_to_all x1, blocking collectives, body(): received = lax.all_to_all(sent, 'lon', 0, 0, tiled=True)  16.5 us
    all_to_all x1, blocking collectives, body(): back = lax.all_to_all(returned, 'lon', 0, 0, tiled=True)  13.5 us
    ppermute x1, starting transfers between devices, body(): across = lax.ppermute(facing, 'lev', [(0, 3), (3, 0), (1, 2), (2, 1)])  7.76 us
    ppermute x1, starting transfers between devices, body(): halo_b = lax.ppermute(out_b, 'lat', [(1, 2), (2, 1)])  7.15 us
    ppermute x1, starting transfers between devices, body(): partner = lax.ppermute(payload, 'lev', [(0, 1), (1, 0), (2, 3), (3, 2)])  6.08 us
    ppermute x1, waiting for transfers between devices, body(): partner = lax.ppermute(payload, 'lev', [(0, 1), (1, 0), (2, 3), (3, 2)])  3.5 us
    ppermute x1, starting transfers between devices, body(): halo_a = lax.ppermute(out_a, 'lat', [(0, 1), (1, 0), (2, 3), (3, 2)])  3.11 us
    unnamed x22, local copies, waits for them, and re-layouts  2.95 us
  transfers between devices with their start and end apart: 4, of which 3 were waited for; matrix products, arithmetic and copies ran while one was open for 0% of the time, Pallas kernels for 0%

commit v1 on v0

v1 whole, which is shorter than its diff:
```python
import math

import jax
import jax.numpy as jnp
import numpy as np
from jax import lax
from jax.experimental import pallas as pl
from jax.experimental.pallas import tpu as pltpu
from jax.sharding import PartitionSpec as P

BINS = 9
LEVELS = 4
TILES = BINS * LEVELS
ROWS = 8
WIDTH = 128
RING = 32
POLE = 4
CIRCLES = POLE * TILES
SHARE = 5
MODES = 128
CIRCLE = RING * WIDTH
PITERS = 3
GAS_CONST = 0.008314
REF_TEMP = 298.0
PRECISE = lax.Precision.HIGHEST
F32 = jnp.float32
VMEM = pl.BlockSpec(memory_space=pltpu.VMEM)
SMEM = pl.BlockSpec(memory_space=pltpu.SMEM)
HBM = pl.BlockSpec(memory_space=pltpu.HBM)
GROUP = 40


def shape(*dims):
    return jax.ShapeDtypeStruct(dims, F32)


def call(kernel, name, outs, in_specs, scratch=()):
    return pl.pallas_call(
        kernel,
        out_shape=outs,
        in_specs=in_specs,
        out_specs=tuple(VMEM for _ in outs),
        scratch_shapes=list(scratch),
        compiler_params=pltpu.CompilerParams(vmem_limit_bytes=16 * 2**20),
        name=name,
    )


def tables():
    modes = np.arange(MODES)

    def pair(columns):
        angle = (columns[:, None] * modes[None, :] % CIRCLE) * (2.0 * math.pi / CIRCLE)
        return np.cos(angle), np.sin(angle)

    inner = np.stack(pair(np.arange(WIDTH))).astype(np.float32)
    first = pair(np.arange(RING) * WIDTH)
    before = pair(np.arange(RING) * WIDTH - 1)
    outer = np.stack([first[0], first[1], first[0] - before[0], first[1] - before[1]])
    return jnp.asarray(inner), jnp.asarray(outer.astype(np.float32))


def iotas():
    lane = lax.broadcasted_iota(jnp.int32, (ROWS, WIDTH), 1)
    row = lax.broadcasted_iota(jnp.int32, (ROWS, WIDTH), 0)
    return lane, row


def spread(row_vector):
    return jnp.broadcast_to(row_vector, (ROWS, WIDTH))


def column(tile, at):
    return jnp.broadcast_to(tile[:, at : at + 1], (ROWS, WIDTH))


def chosen_rows(rows_ref):
    southern = lax.axis_index("lat") >= 2
    return [
        jnp.clip(
            jnp.where(southern, rows_ref[POLE + p] - 3 * ROWS, rows_ref[p]), 0, ROWS - 1
        )
        for p in range(POLE)
    ]


def edge_kernel(burden, merid, out_a, out_b, sems):
    even = lax.axis_index("lat") % 2 == 0
    row_a = jnp.where(even, ROWS - 1, 0)
    row_b = ROWS - 1 - row_a
    copies = []
    for at, (out, row) in enumerate(((out_a, row_a), (out_b, row_b))):
        for half, (source, start, count) in enumerate(((burden, 0, TILES), (merid, TILES, LEVELS))):
            copies.append(
                pltpu.make_async_copy(
                    source.at[:, pl.ds(row, 1), :],
                    out.at[start : start + count],
                    sems.at[2 * at + half],
                )
            )
    for copy in copies:
        copy.start()
    for copy in copies:
        copy.wait()


def setup_kernel(rows_ref, limits_ref, heat, kelvins, weight, code, threshold):
    lane, row = iotas()
    me = lax.axis_index("lon")
    lat = lax.axis_index("lat")
    southern = lat >= 2
    limit = jnp.zeros((ROWS, MODES), jnp.int32)
    for i in range(SHARE):
        p = jnp.minimum((me * SHARE + i) // TILES, POLE - 1)
        kept = limits_ref[p + jnp.where(southern, POLE, 0)]
        limit = jnp.where(row == i, kept, limit)
    weight[...] = jnp.where(lane < limit, jnp.where(lane == 0, 1.0, 2.0), 0.0) * (1.0 / CIRCLE)
    active = (lat == 0) | (lat == 3)
    slot = jnp.full((ROWS, WIDTH), -1, jnp.int32)
    for p, at in enumerate(chosen_rows(rows_ref)):
        slot = jnp.where((row == at) & active, p, slot)
    code[...] = slot
    for k in range(LEVELS):
        inverse = 1.0 / kelvins[k]
        ratio = REF_TEMP * inverse
        slope = (1.0 / REF_TEMP - inverse) * (1.0 / GAS_CONST)
        for b in range(BINS):
            threshold[b * LEVELS + k] = (10.0 ** (b - 2)) * ratio * jnp.exp(heat[b] * slope)


def squeeze_rows(tile, lane):
    packed = jnp.zeros_like(tile)
    for g in range(3):
        moved = pltpu.roll(tile, (5 - 3 * g) % ROWS, 0)
        if g:
            moved = pltpu.roll(moved, GROUP * g, 1)
        packed = jnp.where((lane >= GROUP * g) & (lane < GROUP * (g + 1)), moved, packed)
    return packed


def unsqueeze_rows(packed, row):
    tile = jnp.zeros_like(packed)
    for g in range(3):
        moved = pltpu.roll(packed, (3 * g - 5) % ROWS, 0)
        if g:
            moved = pltpu.roll(moved, WIDTH - GROUP * g, 1)
        tile = jnp.where((row >= 3 * g) & (row < 3 * g + 3), moved, tile)
    return tile


def advect_kernel(rows_ref, burden, zonal, merid, halo_a, partial, sent, edges, packs):
    lane, row = iotas()
    lat = lax.axis_index("lat")
    even = lat % 2 == 0
    first_row = (row == 0) & (lat == 0)
    west_edge = jnp.zeros((ROWS, WIDTH), F32)
    east_edge = jnp.zeros((ROWS, WIDTH), F32)
    face_edge = jnp.zeros((ROWS, WIDTH), F32)
    for k in range(LEVELS):
        face = zonal[k]
        inner = jnp.where(lane == 0, 0.0, face)
        up, down = jnp.maximum(inner, 0.0), jnp.minimum(inner, 0.0)
        south = jnp.where(first_row, 0.0, merid[k])
        south_up, south_down = jnp.maximum(south, 0.0), jnp.minimum(south, 0.0)
        north = spread(jnp.where(even, halo_a[TILES + k], 0.0))
        north_up, north_down = jnp.maximum(north, 0.0), jnp.minimum(north, 0.0)
        face_edge = jnp.where((lane < TILES) & (lane % LEVELS == k), column(face, 0), face_edge)
        for b in range(BINS):
            t = b * LEVELS + k
            tile = burden[t]
            beside = halo_a[t]
            below, above = jnp.where(even, 0.0, beside), jnp.where(even, beside, 0.0)
            west = up * pltpu.roll(tile, 1, 1) + down * tile
            below_cells = jnp.where(row == 0, spread(below), pltpu.roll(tile, 1, 0))
            from_south = south_up * below_cells + south_down * tile
            to_north = jnp.where(
                row == ROWS - 1,
                north_up * tile + north_down * spread(above),
                pltpu.roll(from_south, ROWS - 1, 0),
            )
            partial[t] = (
                tile + west - pltpu.roll(west, WIDTH - 1, 1) + from_south - to_north
            )
            west_edge = jnp.where(lane == t, column(tile, 0), west_edge)
            east_edge = jnp.where(lane == t, column(tile, WIDTH - 1), east_edge)
    edges[0] = east_edge
    edges[1] = west_edge
    edges[2] = face_edge
    packs[0] = squeeze_rows(east_edge, lane)
    packs[1] = squeeze_rows(
        jnp.where(lane < TILES, west_edge, pltpu.roll(face_edge, TILES, 1)), lane
    )
    rows = chosen_rows(rows_ref)
    low = jnp.zeros((ROWS, WIDTH), F32)
    high = jnp.zeros((ROWS, WIDTH), F32)
    for p in range(POLE):
        picked = [edges[e, pl.ds(rows[p], 1), :] for e in range(3)]
        tile = jnp.where(row == 5, spread(picked[0]), jnp.where(row == 6, spread(picked[1]), spread(picked[2])))
        start = TILES * p
        moved = pltpu.roll(tile, start, 1) if start else tile
        low = jnp.where((lane >= start) & (lane < start + TILES), moved, low)
        if start + TILES > 100:
            moved = pltpu.roll(tile, (start - 100) % WIDTH, 1)
            high = jnp.where((lane >= start - 100) & (lane < start - 100 + TILES), moved, high)
    for j in range(RING):
        start = SHARE * j
        source, offset = (low, start) if start + SHARE <= WIDTH else (high, start - 100)
        moved = pltpu.roll(source, (WIDTH - offset) % WIDTH, 1) if offset else source
        sent[j, SHARE:, :] = moved[SHARE:]
        for i in range(SHARE):
            n = start + i
            if n < CIRCLES:
                sent[j, i : i + 1, :] = partial[n % TILES, pl.ds(rows[n // TILES], 1), :]
            else:
                sent[j, i : i + 1, :] = jnp.zeros((1, WIDTH), F32)


def filter_kernel(received, packs, inner, outer, weight_ref, returned, parts):
    me = lax.axis_index("lon")
    block = received[...]
    cosine, sine = inner[0], inner[1]
    flat = block.reshape(RING * ROWS, WIDTH)
    parts[...] = jnp.dot(
        flat,
        jnp.concatenate([cosine, sine], axis=1),
        precision=PRECISE,
        preferred_element_type=F32,
    )
    cosine_part = jnp.zeros((ROWS, MODES), F32)
    sine_part = jnp.zeros((ROWS, MODES), F32)
    for q in range(RING):
        c, s = outer[0, q : q + 1, :], outer[1, q : q + 1, :]
        own_c = parts[ROWS * q : ROWS * (q + 1), :MODES]
        own_s = parts[ROWS * q : ROWS * (q + 1), MODES:]
        cosine_part += c * own_c - s * own_s
        sine_part += s * own_c + c * own_s
    east_cells = received[:, 5, :]
    west_cells = received[:, 6, :]
    faces = received[:, 7, :]
    beyond = pltpu.roll(east_cells, 1, 0)
    flux = jnp.maximum(faces, 0.0) * beyond + jnp.minimum(faces, 0.0) * west_cells
    flux_lane = lax.broadcasted_iota(jnp.int32, flux.shape, 1)
    flux = jnp.where(flux_lane < SHARE, flux, 0.0)
    edge = lax.dot_general(
        flux,
        jnp.concatenate([outer[2], outer[3]], axis=1),
        (((0,), (0,)), ((), ())),
        precision=PRECISE,
        preferred_element_type=F32,
    )
    cosine_part += edge[:ROWS, :MODES]
    sine_part += edge[:ROWS, MODES:]
    weight = weight_ref[...]
    cosine_part *= weight
    sine_part *= weight
    for q in range(RING):
        c, s = outer[0, q : q + 1, :], outer[1, q : q + 1, :]
        parts[ROWS * q : ROWS * (q + 1), :MODES] = cosine_part * c + sine_part * s
        parts[ROWS * q : ROWS * (q + 1), MODES:] = sine_part * c - cosine_part * s
    smooth = jnp.dot(
        parts[...],
        jnp.concatenate([cosine, sine], axis=0),
        precision=PRECISE,
        preferred_element_type=F32,
    )
    returned[...] = smooth.reshape(RING, ROWS, WIDTH)
    returned[(me + 1) % RING, SHARE:, :] = packs[0, SHARE:, :]
    returned[(me + RING - 1) % RING, SHARE:, :] = packs[1, SHARE:, :]


def mend_kernel(burden, merid, halo_b, partial, mended):
    lane, row = iotas()
    even = lax.axis_index("lat") % 2 == 0
    edge = row == jnp.where(even, 0, ROWS - 1)
    for k in range(LEVELS):
        beyond = halo_b[TILES + k]
        face = jnp.where(even, merid[k], spread(beyond))
        up, down = jnp.maximum(face, 0.0), jnp.minimum(face, 0.0)
        for b in range(BINS):
            t = b * LEVELS + k
            cells = spread(halo_b[t])
            flux = jnp.where(even, up * cells, -(up * burden[t] + down * cells))
            mended[t] = partial[t] + jnp.where(edge, flux, 0.0)


def modes_kernel(pair, across, rising, falling, levels, rise, fall):
    me = lax.axis_index("lev")
    bottom = me < 2
    for k in range(2 * LEVELS):
        levels[k] = jnp.where(bottom, pair[k], across[k])
        levels[2 * LEVELS + k] = jnp.where(bottom, across[k], pair[k])
    depth = 4 * LEVELS
    inverse = [None] + [1.0 / levels[k] for k in range(1, depth)]
    up = jnp.ones((ROWS, WIDTH), F32)
    flux = up
    rise[0] = up
    for k in range(1, depth):
        up = up + flux * inverse[k]
        flux = flux + up
        rise[k] = up
    down = 1.0 / flux
    fall[depth - 1] = down
    flux = down
    for k in range(depth - 1, 0, -1):
        down = down + flux * inverse[k]
        flux = flux + down
        fall[k - 1] = down
    rising[...] = rise[pl.ds(LEVELS * me, LEVELS)]
    falling[...] = fall[pl.ds(LEVELS * me, LEVELS)]


def join_kernel(own, other, pair):
    lower = lax.axis_index("lev") % 2 == 0
    for k in range(LEVELS):
        pair[k] = jnp.where(lower, own[k], other[k])
        pair[LEVELS + k] = jnp.where(lower, other[k], own[k])


def column_kernel(mended, edges, back, code, rising, falling, local, outward):
    lane, row = iotas()
    me = lax.axis_index("lon")
    lev = lax.axis_index("lev")
    east_own, west_own, face_own = edges[0], edges[1], edges[2]
    from_west = unsqueeze_rows(back[(me + RING - 1) % RING], row)
    from_east = unsqueeze_rows(back[(me + 1) % RING], row)
    four = jnp.where(lane < LEVELS, pltpu.roll(from_east, WIDTH - TILES, 1), 0.0)
    eight = four + pltpu.roll(four, 4, 1)
    sixteen = eight + pltpu.roll(eight, 8, 1)
    face_next = sixteen + pltpu.roll(sixteen, 16, 1) + pltpu.roll(four, 32, 1)
    flux_in = jnp.maximum(face_own, 0.0) * from_west + jnp.minimum(face_own, 0.0) * west_own
    flux_out = jnp.maximum(face_next, 0.0) * east_own + jnp.minimum(face_next, 0.0) * from_east
    slot = code[...]
    here = [slot == p for p in range(POLE)]
    for b in range(BINS):
        source = []
        for k in range(LEVELS):
            t = b * LEVELS + k
            value = (
                mended[t]
                + jnp.where(lane == 0, column(flux_in, t), 0.0)
                - jnp.where(lane == WIDTH - 1, column(flux_out, t), 0.0)
            )
            for p in range(POLE):
                n = p * TILES + t
                smooth = back[n // SHARE, n % SHARE : n % SHARE + 1, :]
                value = jnp.where(here[p], spread(smooth), value)
            source.append(value)
        before = []
        total = jnp.zeros((ROWS, WIDTH), F32)
        for k in range(LEVELS):
            total = total + rising[k] * source[k]
            before.append(falling[k] * total)
        after = jnp.zeros((ROWS, WIDTH), F32)
        for k in range(LEVELS - 1, -1, -1):
            local[b * LEVELS + k] = before[k] + rising[k] * after
            after = after + falling[k] * source[k]
        for other in range(4):
            outward[other, b] = jnp.where(lev < other, total, after)


def phase_kernel(inward, local, rising, falling, threshold, inert, condensed, gas):
    lev = lax.axis_index("lev")
    from_below, from_above = [], []
    for b in range(BINS):
        below = jnp.zeros((ROWS, WIDTH), F32)
        above = jnp.zeros((ROWS, WIDTH), F32)
        for other in range(4):
            below = below + jnp.where(other < lev, inward[other, b], 0.0)
            above = above + jnp.where(other > lev, inward[other, b], 0.0)
        from_below.append(below)
        from_above.append(above)
    for k in range(LEVELS):
        up, down, emitted = rising[k], falling[k], inert[k]
        totals = [local[b * LEVELS + k] + down * from_below[b] + up * from_above[b] for b in range(BINS)]
        limit = [threshold[b * LEVELS + k] for b in range(BINS)]
        organic = emitted
        for _ in range(PITERS):
            held = totals[0] / (organic + limit[0])
            for b in range(1, BINS):
                held = held + totals[b] / (organic + limit[b])
            organic = emitted + organic * held
        for b in range(BINS):
            particle = totals[b] * (organic / (organic + limit[b]))
            condensed[b * LEVELS + k] = particle
            gas[b * LEVELS + k] = totals[b] - particle


def body(
    bin_burden,
    zonal_cfl_ratio,
    meridional_cfl_ratio,
    thermal_kelvins,
    diffusion_coefficient,
    inert_emitted_aerosol,
    heat_of_evaporation,
    damped_parallels,
    preserved_harmonic_limits,
):
    burden = bin_burden.reshape(TILES, ROWS, WIDTH)
    inner, outer = tables()
    field = shape(TILES, ROWS, WIDTH)
    tile = (ROWS, WIDTH)
    swap = [(0, 1), (1, 0), (2, 3), (3, 2)]
    cross = [(0, 3), (3, 0), (1, 2), (2, 1)]
    out_a, out_b = call(
        edge_kernel,
        "edge",
        (shape(GROUP, 1, WIDTH), shape(GROUP, 1, WIDTH)),
        [HBM] * 2,
        [pltpu.SemaphoreType.DMA((4,))],
    )(burden, meridional_cfl_ratio)
    halo_a = lax.ppermute(out_a, "lat", swap)
    weight, code, threshold = call(
        setup_kernel,
        "setup",
        (shape(*tile), jax.ShapeDtypeStruct(tile, jnp.int32), field),
        [SMEM] * 3 + [VMEM],
    )(damped_parallels, preserved_harmonic_limits, heat_of_evaporation, thermal_kelvins)
    partial, sent, edges, packs = call(
        advect_kernel,
        "advect",
        (field, shape(RING, *tile), shape(3, *tile), shape(2, *tile)),
        [SMEM] + [VMEM] * 4,
    )(damped_parallels, burden, zonal_cfl_ratio, meridional_cfl_ratio, halo_a)
    sent, out_b, mixing = lax.optimization_barrier((sent, out_b, diffusion_coefficient))
    received = lax.all_to_all(sent, "lon", 0, 0, tiled=True)
    halo_b = lax.ppermute(out_b, "lat", [(1, 2), (2, 1)])
    pair = call(join_kernel, "join", (shape(2 * LEVELS, *tile),), [VMEM] * 2)(
        mixing, lax.ppermute(mixing, "lev", swap)
    )[0]
    mended = call(mend_kernel, "mend", (field,), [VMEM] * 4)(
        burden, meridional_cfl_ratio, halo_b, partial
    )[0]
    returned = call(
        filter_kernel,
        "filter",
        (shape(RING, *tile),),
        [VMEM] * 5,
        [pltpu.VMEM((RING * ROWS, 2 * MODES), F32)],
    )(received, packs, inner, outer, weight)[0]
    returned, pair = lax.optimization_barrier((returned, pair))
    rising, falling = call(
        modes_kernel,
        "modes",
        (shape(LEVELS, *tile), shape(LEVELS, *tile)),
        [VMEM] * 2,
        [pltpu.VMEM((4 * LEVELS, *tile), F32)] * 3,
    )(pair, lax.ppermute(pair, "lev", cross))
    back = lax.all_to_all(returned, "lon", 0, 0, tiled=True)
    local, outward = call(
        column_kernel, "column", (field, shape(4, BINS, *tile)), [VMEM] * 6
    )(mended, edges, back, code, rising, falling)
    condensed, gas = call(phase_kernel, "phase", (field, field), [VMEM] * 6)(
        lax.all_to_all(outward, "lev", 0, 0, tiled=True),
        local,
        rising,
        falling,
        threshold,
        inert_emitted_aerosol,
    )
    return condensed.reshape(bin_burden.shape), gas.reshape(bin_burden.shape)


def solution(mesh):
    block = P("lev", "lat", "lon")
    binned = P(None, "lev", "lat", "lon")
    return jax.shard_map(
        body,
        mesh=mesh,
        in_specs=(binned, block, block, block, block, block, P(), P(), P()),
        out_specs=(binned, binned),
        check_vma=False,
    )
```

time: 71.9 us -> 66.6 us (0.926)
  blocking collectives: 30 us -> 12.2 us
  starting transfers between devices: 24.1 us -> 36.1 us
  waiting for transfers between devices: 7.25 us -> 9.33 us
  local copies, waits for them, and re-layouts: 2.95 us -> 1.67 us
    all_to_all x2 -> x1, blocking collectives: 30 us -> 12.2 us  [body(): lax.all_to_all(outward, 'lev', 0, 0, tiled=True)]
    all_to_all x0 -> x2, starting transfers between devices: none -> 15.5 us  [the longest x1 9.44 us: body(): received = lax.all_to_all(sent, 'lon', 0, 0, tiled=True)]
    ppermute x1, starting transfers between devices: 7.15 us -> 2.44 us  [body(): halo_b = lax.ppermute(out_b, 'lat', [(1, 2), (2, 1)])]
    all_to_all x0 -> x2, waiting for transfers between devices: none -> 2.45 us  [the longest x1 2.45 us: body(): received = lax.all_to_all(sent, 'lon', 0, 0, tiled=True)]
    ppermute x3, waiting for transfers between devices: 5.51 us -> 3.65 us  [the longest x1 2.56 us: body(): halo_a = lax.ppermute(out_a, 'lat', swap)]
    ppermute x1, waiting for transfers between devices: 1.74 us -> 3.23 us  [body(): halo_b = lax.ppermute(out_b, 'lat', [(1, 2), (2, 1)])]
    unnamed x22 -> x26, local copies, waits for them, and re-layouts: 2.95 us -> 1.67 us
    ppermute x3, starting transfers between devices: 16.9 us -> 18.1 us  [the longest x1 8.82 us: body(): lax.ppermute(pair, 'lev', cross)]
  transfers between devices with their start and end apart: 4 -> 6, of which waited for: 3 -> 4; matrix products, arithmetic and copies ran while one was open for 0% -> 0% of each run, Pallas kernels for 0% -> 1%
where the time goes in v1:
time: 66.6 us; the launch traced here: 66 us
  starting transfers between devices  36.1 us (54%)
  blocking collectives  12.2 us (18%)
  waiting for transfers between devices  9.33 us (14%)
  Pallas kernels  5.93 us (9%)
  local copies, waits for them, and re-layouts  1.67 us (3%)
  between operations  0.81 us (1%)
    all_to_all x1, blocking collectives, body(): lax.all_to_all(outward, 'lev', 0, 0, tiled=True)  12.2 us
    all_to_all x1, starting transfers between devices, body(): received = lax.all_to_all(sent, 'lon', 0, 0, tiled=True)  9.44 us
    ppermute x1, starting transfers between devices, body(): lax.ppermute(pair, 'lev', cross)  8.82 us
    ppermute x1, starting transfers between devices, body(): lax.ppermute(mixing, 'lev', swap)  6.22 us
    all_to_all x1, starting transfers between devices, body(): back = lax.all_to_all(returned, 'lon', 0, 0, tiled=True)  6.05 us
    ppermute x1, waiting for transfers between devices, body(): halo_b = lax.ppermute(out_b, 'lat', [(1, 2), (2, 1)])  3.23 us
    ppermute x1, starting transfers between devices, body(): halo_a = lax.ppermute(out_a, 'lat', swap)  3.11 us
    ppermute x1, waiting for transfers between devices, body(): halo_a = lax.ppermute(out_a, 'lat', swap)  2.56 us
  transfers between devices with their start and end apart: 6, of which 4 were waited for; matrix products, arithmetic and copies ran while one was open for 0% of the time, Pallas kernels for 1%

profile of v1, /device:TPU:4, one launch (start us, length us, event | category | flops | bytes accessed | tf_op | source)
XLA Modules:
  0.0 66.0 jit_solution(15311393663749502863)
XLA Ops:
  0.6 0.0 copy-start
  0.6 0.9 %copy-done = f32[9,4,8,128]{3,2,1,0:T(8,128)S(1)} copy-done((f32[9,4,8,128]{3,2,1,0:T(8,128)S(1)}, f32[9,4,8,128]{3,2,1,0:T(8,128)}, u32[]{:S(2)}) %copy-start) | copy-done | bytes 147480
  1.5 0.0 copy-start.2
  1.5 0.7 %copy-done.2 = f32[4,8,128]{2,1,0:T(8,128)S(1)} copy-done((f32[4,8,128]{2,1,0:T(8,128)S(1)}, f32[4,8,128]{2,1,0:T(8,128)}, u32[]{:S(2)}) %copy-start.2) | copy-done | bytes 16408
  2.3 0.0 copy-start.6
  2.3 0.1 edge.1
  2.3 0.0 copy-start.10
  2.4 3.1 %collective-permute-start = (f32[40,1,128]{2,1,0:T(1,128)S(1)}, f32[40,1,128]{2,1,0:T(1,128)S(1)}, u32[]{:S(2)}, u32[]{:S(2)}) collective-permute-start(f32[40,1,128]{2,1,0:T(1,128)S(1)} %get-tuple-element.22), channel_id=1, source_target_pairs={{0,4},{4,0},{8,12},{12,8},{1,5},{5,1},{9,13},{13,9},{2,6},{6,2},{1... | collective-permute-start | bytes 61448 | tf_op jit(solution)/shard_map/ppermute | solution.py:412
  5.5 2.6 %collective-permute-done.halo_a = f32[40,1,128]{2,1,0:T(1,128)S(1)} collective-permute-done((f32[40,1,128]{2,1,0:T(1,128)S(1)}, f32[40,1,128]{2,1,0:T(1,128)S(1)}, u32[]{:S(2)}, u32[]{:S(2)}) %collective-permute-start) | collective-permute-done | bytes 20512 | tf_op jit(solution)/shard_map/ppermute | solution.py:412
  8.0 0.0 copy-done.6
  8.0 0.0 copy-done.10
  8.0 2.0 %advect.1 = (f32[36,8,128]{2,1,0:T(8,128)S(1)}, f32[32,8,128]{2,1,0:T(8,128)}, f32[3,8,128]{2,1,0:T(8,128)S(1)}, f32[2,8,128]{2,1,0:T(8,128)S(1)}) custom-call(s32[8]{0:T(128)S(1)} %copy-done.10, f32[36,8,128]{2,1,0:T(8,128)S(1)} %bitcast.4, f32[4,8,128]{2,1,0:T(8,128)S(1)} %copy-done.6, f32[4,8,128]{2,1,0:T(8,128)S(1)} %copy-done.2, ...), custom_call_target="tpu_custom_call" | custom-call | tf_op jit(solution)/shard_map/advect/pallas_call | solution.py:419
  10.0 0.0 copy-start.9
  10.0 0.0 copy-start.8
  10.0 0.0 copy-start.11
  10.0 0.0 copy-start.12
  10.0 0.0 copy-start.4
  10.0 9.4 %all-to-all-start = ((f32[32,8,128]{2,1,0:T(8,128)}), f32[32,8,128]{2,1,0:T(8,128)S(1)}, u32[]{:S(2)}, u32[]{:S(2)}) async-start(f32[32,8,128]{2,1,0:T(8,128)} %get-tuple-element.28), calls=%async_computation | async-start | bytes 262144 | tf_op jit(solution)/shard_map/all_to_all | solution.py:426
  19.5 0.0 copy-done.9
  19.5 0.0 copy-start.5
  19.5 6.2 %collective-permute-start.2 = (f32[4,8,128]{2,1,0:T(8,128)S(1)}, f32[4,8,128]{2,1,0:T(8,128)S(1)}, u32[]{:S(2)}, u32[]{:S(2)}) collective-permute-start(f32[4,8,128]{2,1,0:T(8,128)S(1)} %copy-done.9), channel_id=1, source_target_pairs={{0,1},{1,0},{2,3},{3,2},{4,5},{5,4},{6,7},{7,6},{8,9},{9,8},{10,11... | collective-permute-start | bytes 49160 | tf_op jit(solution)/shard_map/ppermute | solution.py:429
  25.7 0.0 copy-done.8
  25.8 0.0 copy-done.11
  25.8 0.0 copy-done.12
  25.8 0.6 setup.1
  26.4 1.1 %collective-permute-done.2.other = f32[4,8,128]{2,1,0:T(8,128)S(1)} collective-permute-done((f32[4,8,128]{2,1,0:T(8,128)S(1)}, f32[4,8,128]{2,1,0:T(8,128)S(1)}, u32[]{:S(2)}, u32[]{:S(2)}) %collective-permute-start.2) | collective-permute-done | bytes 16416 | tf_op jit(solution)/shard_map/ppermute | solution.py:429
  27.5 2.5 %all-to-all-done.received = f32[32,8,128]{2,1,0:T(8,128)S(1)} async-done(((f32[32,8,128]{2,1,0:T(8,128)}), f32[32,8,128]{2,1,0:T(8,128)S(1)}, u32[]{:S(2)}, u32[]{:S(2)}) %all-to-all-start) | async-done | bytes 131104 | tf_op jit(solution)/shard_map/all_to_all | solution.py:426
  29.9 0.0 copy-done.4
  30.0 0.0 copy-done.5
  30.0 1.7 %filter.1 = f32[32,8,128]{2,1,0:T(8,128)} custom-call(f32[32,8,128]{2,1,0:T(8,128)S(1)} %all-to-all-done.received, f32[2,8,128]{2,1,0:T(8,128)S(1)} %get-tuple-element.29.packs, f32[2,128,128]{2,1,0:T(8,128)S(1)} %copy-done.4, f32[4,32,128]{2,1,0:T(8,128)S(1)} %copy-done.5, f32[8,128]{1,0:T(8,128)S(1)} %get-tuple-element.30.weight_ref), custom_call_target="tpu_custom_call" | custom-call | tf_op jit(solution)/shard_map/filter/pallas_call | solution.py:434
  31.6 0.0 copy-start.1
  31.6 0.0 copy-start.3
  31.6 6.1 %all-to-all-start.1 = ((f32[32,8,128]{2,1,0:T(8,128)}), f32[32,8,128]{2,1,0:T(8,128)S(1)}, u32[]{:S(2)}, u32[]{:S(2)}) async-start(f32[32,8,128]{2,1,0:T(8,128)} %filter.1), calls=%async_computation.1 | async-start | bytes 262144 | tf_op jit(solution)/shard_map/all_to_all | solution.py:449
  37.7 8.8 %collective-permute-start.3 = (f32[8,8,128]{2,1,0:T(8,128)S(1)}, f32[8,8,128]{2,1,0:T(8,128)S(1)}, u32[]{:S(2)}, u32[]{:S(2)}) collective-permute-start(f32[8,8,128]{2,1,0:T(8,128)S(1)} %join.1.pair), channel_id=1, source_target_pairs={{0,3},{3,0},{1,2},{2,1},{4,7},{7,4},{5,6},{6,5},{8,11},{11,8},{9,1... | collective-permute-start | bytes 98312 | tf_op jit(solution)/shard_map/ppermute | solution.py:448
  46.5 2.4 %collective-permute-start.1 = (f32[40,1,128]{2,1,0:T(1,128)S(1)}, f32[40,1,128]{2,1,0:T(1,128)S(1)}, u32[]{:S(2)}, u32[]{:S(2)}) collective-permute-start(f32[40,1,128]{2,1,0:T(1,128)S(1)} %get-tuple-element.25), channel_id=1, source_target_pairs={{4,8},{8,4},{5,9},{9,5},{6,10},{10,6},{7,11},{11,7},{20,24},{24,20... | collective-permute-start | bytes 61448 | tf_op jit(solution)/shard_map/ppermute | solution.py:427
  49.0 3.2 %collective-permute-done.1.halo_b = f32[40,1,128]{2,1,0:T(1,128)S(1)} collective-permute-done((f32[40,1,128]{2,1,0:T(1,128)S(1)}, f32[40,1,128]{2,1,0:T(1,128)S(1)}, u32[]{:S(2)}, u32[]{:S(2)}) %collective-permute-start.1) | collective-permute-done | bytes 20512 | tf_op jit(solution)/shard_map/ppermute | solution.py:427
  52.2 0.0 copy-done.1
  52.2 0.0 copy-done.3
  52.2 0.1 mend.1.mended
  52.3 0.0 collective-permute-done.3.across
  52.3 0.1 modes.1
  52.4 0.0 all-to-all-done.1.back
  52.4 0.5 column.1
  52.9 0.0 copy-start.7
  52.9 12.2 %all_to_all.15.inward = f32[4,9,8,128]{3,2,1,0:T(8,128)S(1)} all-to-all(f32[4,9,8,128]{3,2,1,0:T(8,128)S(1)} %get-tuple-element.37), channel_id=1, replica_groups=mesh['lon'=32,'lat'=4,'lev'=4] {'lev'}, dimensions={0} | all-to-all | bytes 294912 | tf_op jit(solution)/shard_map/all_to_all | solution.py:454
  65.1 0.0 copy-done.7
  65.1 0.9 %phase.1 = (f32[36,8,128]{2,1,0:T(8,128)}, f32[36,8,128]{2,1,0:T(8,128)}) custom-call(f32[4,9,8,128]{3,2,1,0:T(8,128)S(1)} %all_to_all.15.inward, f32[36,8,128]{2,1,0:T(8,128)S(1)} %get-tuple-element.38.local, f32[4,8,128]{2,1,0:T(8,128)S(1)} %get-tuple-element.35.rising, f32[4,8,128]{2,1,0:T(8,128)S(1)} %get-tuple-element.36.falling, ...), custom_call_target="tpu_custom_call" | custom-call | tf_op jit(solution)/shard_map/phase/pallas_call | solution.py:453
  (1 shorter events, 0.0 us)
Async XLA Ops:
  0.6 0.9 %copy-start = (f32[9,4,8,128]{3,2,1,0:T(8,128)S(1)}, f32[9,4,8,128]{3,2,1,0:T(8,128)}, u32[]{:S(2)}) copy-start(f32[9,4,8,128]{3,2,1,0:T(8,128)} %param.11) | copy-start | bytes 442372
  1.5 0.7 %copy-start.2 = (f32[4,8,128]{2,1,0:T(8,128)S(1)}, f32[4,8,128]{2,1,0:T(8,128)}, u32[]{:S(2)}) copy-start(f32[4,8,128]{2,1,0:T(8,128)} %merid.5) | copy-start | bytes 49156
  2.3 5.8 %copy-start.6 = (f32[4,8,128]{2,1,0:T(8,128)S(1)}, f32[4,8,128]{2,1,0:T(8,128)}, u32[]{:S(2)}) copy-start(f32[4,8,128]{2,1,0:T(8,128)} %zonal.1) | copy-start | bytes 49156
  2.3 5.7 %copy-start.10 = (s32[8]{0:T(128)S(1)}, s32[8]{0:T(128)}, u32[]{:S(2)}) copy-start(s32[8]{0:T(128)} %rows_ref.3) | copy-start | bytes 100
  2.4 5.7 %collective-permute-start = (f32[40,1,128]{2,1,0:T(1,128)S(1)}, f32[40,1,128]{2,1,0:T(1,128)S(1)}, u32[]{:S(2)}, u32[]{:S(2)}) collective-permute-start(f32[40,1,128]{2,1,0:T(1,128)S(1)} %get-tuple-element.22), channel_id=1, source_target_pairs={{0,4},{4,0},{8,12},{12,8},{1,5},{5,1},{9,13},{13,9},{2,6},{6,2},{1... | collective-permute-start | bytes 61448 | tf_op jit(solution)/shard_map/ppermute | solution.py:412
  10.0 9.5 %copy-start.9 = (f32[4,8,128]{2,1,0:T(8,128)S(1)}, f32[4,8,128]{2,1,0:T(8,128)}, u32[]{:S(2)}) copy-start(f32[4,8,128]{2,1,0:T(8,128)} %own) | copy-start | bytes 49156
  10.0 15.7 %copy-start.8 = (f32[4,8,128]{2,1,0:T(8,128)S(1)}, f32[4,8,128]{2,1,0:T(8,128)}, u32[]{:S(2)}) copy-start(f32[4,8,128]{2,1,0:T(8,128)} %kelvins.1) | copy-start | bytes 49156
  10.0 15.7 %copy-start.11 = (s32[8]{0:T(128)S(1)}, s32[8]{0:T(128)}, u32[]{:S(2)}) copy-start(s32[8]{0:T(128)} %limits_ref.1) | copy-start | bytes 100
  10.0 15.7 %copy-start.12 = (f32[9]{0:T(128)S(1)}, f32[9]{0:T(128)}, u32[]{:S(2)}) copy-start(f32[9]{0:T(128)} %heat.1) | copy-start | bytes 112
  10.0 19.9 %copy-start.4 = (f32[2,128,128]{2,1,0:T(8,128)S(1)}, f32[2,128,128]{2,1,0:T(8,128)}, u32[]{:S(2)}) copy-start(f32[2,128,128]{2,1,0:T(8,128)} %constant.4.clone.inner) | copy-start | bytes 393220
  10.0 19.9 %all-to-all-start = ((f32[32,8,128]{2,1,0:T(8,128)}), f32[32,8,128]{2,1,0:T(8,128)S(1)}, u32[]{:S(2)}, u32[]{:S(2)}) async-start(f32[32,8,128]{2,1,0:T(8,128)} %get-tuple-element.28), calls=%async_computation | async-start | bytes 262144 | tf_op jit(solution)/shard_map/all_to_all | solution.py:426
  19.5 10.5 %copy-start.5 = (f32[4,32,128]{2,1,0:T(8,128)S(1)}, f32[4,32,128]{2,1,0:T(8,128)}, u32[]{:S(2)}) copy-start(f32[4,32,128]{2,1,0:T(8,128)} %constant.5.clone.outer) | copy-start | bytes 196612
  19.5 8.0 %collective-permute-start.2 = (f32[4,8,128]{2,1,0:T(8,128)S(1)}, f32[4,8,128]{2,1,0:T(8,128)S(1)}, u32[]{:S(2)}, u32[]{:S(2)}) collective-permute-start(f32[4,8,128]{2,1,0:T(8,128)S(1)} %copy-done.9), channel_id=1, source_target_pairs={{0,1},{1,0},{2,3},{3,2},{4,5},{5,4},{6,7},{7,6},{8,9},{9,8},{10,11... | collective-permute-start | bytes 49160 | tf_op jit(solution)/shard_map/ppermute | solution.py:429
  31.6 20.6 %copy-start.1 = (f32[9,4,8,128]{3,2,1,0:T(8,128)S(1)}, f32[9,4,8,128]{3,2,1,0:T(8,128)}, u32[]{:S(2)}) copy-start(f32[9,4,8,128]{3,2,1,0:T(8,128)} %param.11) | copy-start | bytes 442372
  31.6 20.6 %copy-start.3 = (f32[4,8,128]{2,1,0:T(8,128)S(1)}, f32[4,8,128]{2,1,0:T(8,128)}, u32[]{:S(2)}) copy-start(f32[4,8,128]{2,1,0:T(8,128)} %merid.5) | copy-start | bytes 49156
  31.6 20.8 %all-to-all-start.1 = ((f32[32,8,128]{2,1,0:T(8,128)}), f32[32,8,128]{2,1,0:T(8,128)S(1)}, u32[]{:S(2)}, u32[]{:S(2)}) async-start(f32[32,8,128]{2,1,0:T(8,128)} %filter.1), calls=%async_computation.1 | async-start | bytes 262144 | tf_op jit(solution)/shard_map/all_to_all | solution.py:449
  37.7 14.6 %collective-permute-start.3 = (f32[8,8,128]{2,1,0:T(8,128)S(1)}, f32[8,8,128]{2,1,0:T(8,128)S(1)}, u32[]{:S(2)}, u32[]{:S(2)}) collective-permute-start(f32[8,8,128]{2,1,0:T(8,128)S(1)} %join.1.pair), channel_id=1, source_target_pairs={{0,3},{3,0},{1,2},{2,1},{4,7},{7,4},{5,6},{6,5},{8,11},{11,8},{9,1... | collective-permute-start | bytes 98312 | tf_op jit(solution)/shard_map/ppermute | solution.py:448
  46.5 5.7 %collective-permute-start.1 = (f32[40,1,128]{2,1,0:T(1,128)S(1)}, f32[40,1,128]{2,1,0:T(1,128)S(1)}, u32[]{:S(2)}, u32[]{:S(2)}) collective-permute-start(f32[40,1,128]{2,1,0:T(1,128)S(1)} %get-tuple-element.25), channel_id=1, source_target_pairs={{4,8},{8,4},{5,9},{9,5},{6,10},{10,6},{7,11},{11,7},{20,24},{24,20... | collective-permute-start | bytes 61448 | tf_op jit(solution)/shard_map/ppermute | solution.py:427
  52.9 12.2 %copy-start.7 = (f32[4,8,128]{2,1,0:T(8,128)S(1)}, f32[4,8,128]{2,1,0:T(8,128)}, u32[]{:S(2)}) copy-start(f32[4,8,128]{2,1,0:T(8,128)} %inert.1) | copy-start | bytes 49156

commit v2 on v0

--- a/solution.py
+++ b/solution.py
@@ -25,7 +25,6 @@
 PRECISE = lax.Precision.HIGHEST
 F32 = jnp.float32
 VMEM = pl.BlockSpec(memory_space=pltpu.VMEM)
-SMEM = pl.BlockSpec(memory_space=pltpu.SMEM)
 GROUP = 40
 
 
@@ -33,13 +32,15 @@
     return jax.ShapeDtypeStruct(dims, F32)
 
 
-def call(kernel, name, outs, in_specs):
+def call(kernel, name, outs, in_specs, scratch=(), flops=10**7):
     return pl.pallas_call(
         kernel,
         out_shape=outs,
         in_specs=in_specs,
         out_specs=tuple(VMEM for _ in outs),
+        scratch_shapes=list(scratch),
         compiler_params=pltpu.CompilerParams(vmem_limit_bytes=16 * 2**20),
+        cost_estimate=pl.CostEstimate(flops=flops, bytes_accessed=10**5, transcendentals=0),
         name=name,
     )
 
@@ -72,27 +73,43 @@
     return jnp.broadcast_to(tile[:, at : at + 1], (ROWS, WIDTH))
 
 
-def chosen_rows(rows_ref):
+def chosen_rows(settings):
     southern = lax.axis_index("lat") >= 2
+    rows = settings[...]
     return [
         jnp.clip(
-            jnp.where(southern, rows_ref[POLE + p] - 3 * ROWS, rows_ref[p]), 0, ROWS - 1
+            jnp.where(southern, rows[0, POLE + p] - 3 * ROWS, rows[0, p]), 0, ROWS - 1
         )
         for p in range(POLE)
     ]
 
 
-def edge_kernel(burden, merid, out_a, out_b):
+def blank_kernel(out):
+    out[...] = jnp.zeros((ROWS, WIDTH), F32)
+
+
+def edge_kernel(blank, rows, limits, burden, merid, out_a, out_b, settings):
+    settings[0:1, : 2 * POLE] = rows[...]
+    settings[1:2, : 2 * POLE] = limits[...]
     even = lax.axis_index("lat") % 2 == 0
     row_a = jnp.where(even, ROWS - 1, 0)
     row_b = ROWS - 1 - row_a
     for t in range(TILES):
-        out_a[t : t + 1, :] = burden[t, pl.ds(row_a, 1), :]
-        out_b[t : t + 1, :] = burden[t, pl.ds(row_b, 1), :]
+        out_a[t] = burden[t, pl.ds(row_a, 1), :]
+        out_b[t] = burden[t, pl.ds(row_b, 1), :]
     for k in range(LEVELS):
-        at = TILES + k
-        out_a[at : at + 1, :] = merid[k, pl.ds(row_a, 1), :]
-        out_b[at : at + 1, :] = merid[k, pl.ds(row_b, 1), :]
+        out_a[TILES + k] = merid[k, pl.ds(row_a, 1), :]
+        out_b[TILES + k] = merid[k, pl.ds(row_b, 1), :]
+
+
+def threshold_kernel(heat, kelvins, threshold):
+    for k in range(LEVELS):
+        inverse = 1.0 / kelvins[k]
+        ratio = REF_TEMP * inverse
+        slope = (1.0 / REF_TEMP - inverse) * (1.0 / GAS_CONST)
+        for b in range(BINS):
+            rise = jnp.broadcast_to(heat[:, b : b + 1], (ROWS, WIDTH))
+            threshold[b * LEVELS + k] = (10.0 ** (b - 2)) * ratio * jnp.exp(rise * slope)
 
 
 def squeeze_rows(tile, lane):
@@ -115,10 +132,9 @@
     return tile
 
 
-def advect_kernel(rows_ref, burden, zonal, merid, halo_a, halo_b, partial, sent, edges, packs):
+def advect_kernel(settings, burden, zonal, merid, partial, edges, packs, faces, weight):
     lane, row = iotas()
     lat = lax.axis_index("lat")
-    even = lat % 2 == 0
     first_row = (row == 0) & (lat == 0)
     west_edge = jnp.zeros((ROWS, WIDTH), F32)
     east_edge = jnp.zeros((ROWS, WIDTH), F32)
@@ -128,24 +144,15 @@
         inner = jnp.where(lane == 0, 0.0, face)
         up, down = jnp.maximum(inner, 0.0), jnp.minimum(inner, 0.0)
         south = jnp.where(first_row, 0.0, merid[k])
-        south_up, south_down = jnp.maximum(south, 0.0), jnp.minimum(south, 0.0)
-        at = TILES + k
-        north = spread(jnp.where(even, halo_a[at : at + 1, :], halo_b[at : at + 1, :]))
-        north_up, north_down = jnp.maximum(north, 0.0), jnp.minimum(north, 0.0)
+        south_up = jnp.where(row == 0, 0.0, jnp.maximum(south, 0.0))
+        south_down = jnp.minimum(south, 0.0)
         face_edge = jnp.where((lane < TILES) & (lane % LEVELS == k), column(face, 0), face_edge)
         for b in range(BINS):
             t = b * LEVELS + k
             tile = burden[t]
-            row_a, row_b = halo_a[t : t + 1, :], halo_b[t : t + 1, :]
-            below, above = jnp.where(even, row_b, row_a), jnp.where(even, row_a, row_b)
             west = up * pltpu.roll(tile, 1, 1) + down * tile
-            below_cells = jnp.where(row == 0, spread(below), pltpu.roll(tile, 1, 0))
-            from_south = south_up * below_cells + south_down * tile
-            to_north = jnp.where(
-                row == ROWS - 1,
-                north_up * tile + north_down * spread(above),
-                pltpu.roll(from_south, ROWS - 1, 0),
-            )
+            from_south = south_up * pltpu.roll(tile, 1, 0) + south_down * tile
+            to_north = jnp.where(row == ROWS - 1, 0.0, pltpu.roll(from_south, ROWS - 1, 0))
             partial[t] = (
                 tile + west - pltpu.roll(west, WIDTH - 1, 1) + from_south - to_north
             )
@@ -158,7 +165,15 @@
     packs[1] = squeeze_rows(
         jnp.where(lane < TILES, west_edge, pltpu.roll(face_edge, TILES, 1)), lane
     )
-    rows = chosen_rows(rows_ref)
+    me = lax.axis_index("lon")
+    southern = lat >= 2
+    number = SHARE * me + row
+    limit = jnp.zeros((ROWS, MODES), jnp.int32)
+    for p in range(POLE):
+        kept = jnp.where(southern, settings[1:2, POLE + p : POLE + p + 1], settings[1:2, p : p + 1])
+        limit = jnp.where(number >= p * TILES, jnp.broadcast_to(kept, (ROWS, MODES)), limit)
+    weight[...] = jnp.where(lane < limit, jnp.where(lane == 0, 1.0, 2.0), 0.0) * (1.0 / CIRCLE)
+    rows = chosen_rows(settings)
     low = jnp.zeros((ROWS, WIDTH), F32)
     high = jnp.zeros((ROWS, WIDTH), F32)
     for p in range(POLE):
@@ -173,20 +188,41 @@
     for j in range(RING):
         start = SHARE * j
         source, offset = (low, start) if start + SHARE <= WIDTH else (high, start - 100)
-        moved = pltpu.roll(source, (WIDTH - offset) % WIDTH, 1) if offset else source
-        sent[j, SHARE:, :] = moved[SHARE:]
+        faces[j] = pltpu.roll(source, (WIDTH - offset) % WIDTH, 1) if offset else source
+
+
+def border(t, k, at_south, row, halo, burden, merid):
+    beyond = spread(halo[TILES + k])
+    cells = spread(halo[t])
+    face = jnp.where(at_south, merid[k], beyond)
+    up, down = jnp.maximum(face, 0.0), jnp.minimum(face, 0.0)
+    flux = jnp.where(at_south, up * cells, -(up * burden[t] + down * cells))
+    return jnp.where(row == jnp.where(at_south, 0, ROWS - 1), flux, 0.0)
+
+
+def pack_kernel(settings, burden, merid, halo_a, halo_b, partial, faces, bordered, sent):
+    lane, row = iotas()
+    odd = lax.axis_index("lat") % 2 == 1
+    for t in range(TILES):
+        k = t % LEVELS
+        bordered[t] = (
+            partial[t]
+            + border(t, k, odd, row, halo_a, burden, merid)
+            + border(t, k, ~odd, row, halo_b, burden, merid)
+        )
+    rows = chosen_rows(settings)
+    for j in range(RING):
+        sent[j, SHARE:, :] = faces[j, SHARE:, :]
         for i in range(SHARE):
-            n = start + i
+            n = SHARE * j + i
             if n < CIRCLES:
-                sent[j, i : i + 1, :] = partial[n % TILES, pl.ds(rows[n // TILES], 1), :]
+                sent[j, i : i + 1, :] = bordered[n % TILES, pl.ds(rows[n // TILES], 1), :]
             else:
                 sent[j, i : i + 1, :] = jnp.zeros((1, WIDTH), F32)
 
 
-def filter_kernel(limits_ref, received, packs, inner, outer, returned, parts):
-    lane, row = iotas()
+def filter_kernel(received, packs, inner, outer, weight_ref, returned, parts):
     me = lax.axis_index("lon")
-    southern = lax.axis_index("lat") >= 2
     block = received[...]
     cosine, sine = inner[0], inner[1]
     flat = block.reshape(RING * ROWS, WIDTH)
@@ -220,12 +256,7 @@
     )
     cosine_part += edge[:ROWS, :MODES]
     sine_part += edge[:ROWS, MODES:]
-    limit = jnp.zeros((ROWS, MODES), jnp.int32)
-    for i in range(SHARE):
-        p = jnp.minimum((me * SHARE + i) // TILES, POLE - 1)
-        kept = limits_ref[p + jnp.where(southern, POLE, 0)]
-        limit = jnp.where(row == i, kept, limit)
-    weight = jnp.where(lane < limit, jnp.where(lane == 0, 1.0, 2.0), 0.0) * (1.0 / CIRCLE)
+    weight = weight_ref[...]
     cosine_part *= weight
     sine_part *= weight
     for q in range(RING):
@@ -243,10 +274,9 @@
     returned[(me + RING - 1) % RING, SHARE:, :] = packs[1, SHARE:, :]
 
 
-def column_kernel(rows_ref, partial, edges, back, diffusion, local, response, payload, filtered):
+def column_kernel(settings, bordered, edges, back, diffusion, local, response, payload):
     lane, row = iotas()
     me = lax.axis_index("lon")
-    lat = lax.axis_index("lat")
     east_own, west_own, face_own = edges[0], edges[1], edges[2]
     from_west = unsqueeze_rows(back[(me + RING - 1) % RING], row)
     from_east = unsqueeze_rows(back[(me + 1) % RING], row)
@@ -256,19 +286,13 @@
     face_next = sixteen + pltpu.roll(sixteen, 16, 1) + pltpu.roll(four, 32, 1)
     flux_in = jnp.maximum(face_own, 0.0) * from_west + jnp.minimum(face_own, 0.0) * west_own
     flux_out = jnp.maximum(face_next, 0.0) * east_own + jnp.minimum(face_next, 0.0) * from_east
-    for t in range(TILES):
-        filtered[t] = (
-            partial[t]
-            + jnp.where(lane == 0, column(flux_in, t), 0.0)
-            - jnp.where(lane == WIDTH - 1, column(flux_out, t), 0.0)
-        )
-    rows = chosen_rows(rows_ref)
-
-    @pl.when((lat == 0) | (lat == 3))
-    def _():
-        for n in range(CIRCLES):
-            filtered[n % TILES, pl.ds(rows[n // TILES], 1), :] = back[n // SHARE, n % SHARE : n % SHARE + 1, :]
-
+    lat = lax.axis_index("lat")
+    active = (lat == 0) | (lat == 3)
+    here = []
+    for p in range(POLE):
+        north, south = settings[0:1, p : p + 1], settings[0:1, POLE + p : POLE + p + 1] - 3 * ROWS
+        chosen = jnp.broadcast_to(jnp.where(lat == 0, north, south), (ROWS, WIDTH))
+        here.append((row == chosen) & active)
     a1, a2, a3 = diffusion[1], diffusion[2], diffusion[3]
     i0 = 1.0 / (1.0 + a1)
     w1 = a1 * i0
@@ -283,20 +307,31 @@
     up2 = w3 * up3
     up1 = w2 * up2
     up0 = w1 * up1
-    d1 = w1
-    d2 = w2 * d1
-    d3 = w3 * d2
-    low3 = d3 * i3
+    d2 = w2 * w1
+    low3 = w3 * d2 * i3
     low2 = d2 * i2 + w3 * low3
-    low1 = d1 * i1 + w2 * low2
+    low1 = w1 * i1 + w2 * low2
     low0 = i0 + w1 * low1
     for at, value in enumerate((low0, low1, low2, low3, up0, up1, up2, up3)):
         response[at] = value
     for b in range(BINS):
-        f0 = filtered[b * LEVELS]
-        f1 = filtered[b * LEVELS + 1] + w1 * f0
-        f2 = filtered[b * LEVELS + 2] + w2 * f1
-        f3 = filtered[b * LEVELS + 3] + w3 * f2
+        source = []
+        for k in range(LEVELS):
+            t = b * LEVELS + k
+            value = (
+                bordered[t]
+                + jnp.where(lane == 0, column(flux_in, t), 0.0)
+                - jnp.where(lane == WIDTH - 1, column(flux_out, t), 0.0)
+            )
+            for p in range(POLE):
+                n = p * TILES + t
+                smooth = back[n // SHARE, n % SHARE : n % SHARE + 1, :]
+                value = jnp.where(here[p], spread(smooth), value)
+            source.append(value)
+        f0 = source[0]
+        f1 = source[1] + w1 * f0
+        f2 = source[2] + w2 * f1
+        f3 = source[3] + w3 * f2
         x3 = f3 * i3
         x2 = f2 * i2 + w3 * x3
         x1 = f1 * i1 + w2 * x2
@@ -339,7 +374,7 @@
         payload[b] = jnp.where(bottom, of_upper(BINS + b), of_lower(b)) + signed * flux
 
 
-def phase_kernel(heat, own, other, inside, local, response, kelvins, inert, condensed, gas):
+def phase_kernel(own, other, inside, local, response, threshold, inert, condensed, gas):
     lev = lax.axis_index("lev")
     lower = lev % 2 == 0
     middle = (lev == 1) | (lev == 2)
@@ -353,23 +388,17 @@
         below.append(jnp.where(lower, open_end, mid))
         above.append(jnp.where(lower, mid, open_end))
     for k in range(LEVELS):
-        inverse = 1.0 / kelvins[k]
-        ratio = REF_TEMP * inverse
-        slope = (1.0 / REF_TEMP - inverse) * (1.0 / GAS_CONST)
-        low, up = response[k], response[LEVELS + k]
-        emitted = inert[k]
-        totals, threshold = [], []
-        for b in range(BINS):
-            totals.append(local[b * LEVELS + k] + low * below[b] - up * above[b])
-            threshold.append((10.0 ** (b - 2)) * ratio * jnp.exp(heat[b] * slope))
+        low, up, emitted = response[k], response[LEVELS + k], inert[k]
+        totals = [local[b * LEVELS + k] + low * below[b] - up * above[b] for b in range(BINS)]
+        limit = [threshold[b * LEVELS + k] for b in range(BINS)]
         organic = emitted
         for _ in range(PITERS):
-            held = emitted
-            for b in range(BINS):
-                held = held + totals[b] * (organic / (organic + threshold[b]))
-            organic = held
+            held = totals[0] / (organic + limit[0])
+            for b in range(1, BINS):
+                held = held + totals[b] / (organic + limit[b])
+            organic = emitted + organic * held
         for b in range(BINS):
-            particle = totals[b] * (organic / (organic + threshold[b]))
+            particle = totals[b] * (organic / (organic + limit[b]))
             condensed[b * LEVELS + k] = particle
             gas[b * LEVELS + k] = totals[b] - particle
 
@@ -388,48 +417,68 @@
     burden = bin_burden.reshape(TILES, ROWS, WIDTH)
     inner, outer = tables()
     field = shape(TILES, ROWS, WIDTH)
-    out_a, out_b = call(
-        edge_kernel, "edge", (shape(GROUP, WIDTH), shape(GROUP, WIDTH)), [VMEM] * 2
-    )(burden, meridional_cfl_ratio)
-    halo_a = lax.ppermute(out_a, "lat", [(0, 1), (1, 0), (2, 3), (3, 2)])
+    tile = (ROWS, WIDTH)
+    swap = [(0, 1), (1, 0), (2, 3), (3, 2)]
+    cross = [(0, 3), (3, 0), (1, 2), (2, 1)]
+    out_a, out_b, settings = call(
+        edge_kernel,
+        "edge",
+        (shape(GROUP, 1, WIDTH), shape(GROUP, 1, WIDTH), jax.ShapeDtypeStruct(tile, jnp.int32)),
+        [VMEM] * 5,
+    )(
+        call(blank_kernel, "blank", (shape(*tile),), [], flops=4 * 10**9)()[0],
+        damped_parallels.reshape(1, 2 * POLE),
+        preserved_harmonic_limits.reshape(1, 2 * POLE),
+        burden,
+        meridional_cfl_ratio,
+    )
+    halo_a = lax.ppermute(out_a, "lat", swap)
     halo_b = lax.ppermute(out_b, "lat", [(1, 2), (2, 1)])
-    partial, sent, edges, packs = call(
+    partial, edges, packs, faces, weight = call(
         advect_kernel,
         "advect",
-        (field, shape(RING, ROWS, WIDTH), shape(3, ROWS, WIDTH), shape(2, ROWS, WIDTH)),
-        [SMEM] + [VMEM] * 5,
-    )(damped_parallels, burden, zonal_cfl_ratio, meridional_cfl_ratio, halo_a, halo_b)
+        (field, shape(3, *tile), shape(2, *tile), shape(RING, *tile), shape(*tile)),
+        [VMEM] * 4,
+    )(settings, burden, zonal_cfl_ratio, meridional_cfl_ratio)
+    halo_a, partial, faces = lax.optimization_barrier((halo_a, partial, faces))
+    bordered, sent = call(
+        pack_kernel, "pack", (field, shape(RING, *tile)), [VMEM] * 7
+    )(settings, burden, meridional_cfl_ratio, halo_a, halo_b, partial, faces)
     received = lax.all_to_all(sent, "lon", 0, 0, tiled=True)
-    returned, _ = call(
+    returned = call(
         filter_kernel,
         "filter",
-        (shape(RING, ROWS, WIDTH), shape(RING * ROWS, 2 * MODES)),
-        [SMEM] + [VMEM] * 4,
-    )(preserved_harmonic_limits, received, packs, inner, outer)
+        (shape(RING, *tile),),
+        [VMEM] * 5,
+        [pltpu.VMEM((RING * ROWS, 2 * MODES), F32)],
+    )(received, packs, inner, outer, weight)[0]
     back = lax.all_to_all(returned, "lon", 0, 0, tiled=True)
-    ends = shape(2 * BINS + 4, ROWS, WIDTH)
-    local, response, payload, _ = call(
+    count = 2 * BINS + 4
+    local, response, payload = call(
         column_kernel,
         "column",
-        (field, shape(2 * LEVELS, ROWS, WIDTH), ends, field),
-        [SMEM] + [VMEM] * 4,
-    )(damped_parallels, partial, edges, back, diffusion_coefficient)
-    partner = lax.ppermute(payload, "lev", [(0, 1), (1, 0), (2, 3), (3, 2)])
+        (field, shape(2 * LEVELS, *tile), shape(count, *tile)),
+        [VMEM] * 5,
+    )(settings, bordered, edges, back, diffusion_coefficient)
+    payload, kelvins = lax.optimization_barrier((payload, thermal_kelvins))
+    partner = lax.ppermute(payload, "lev", swap)
+    threshold = call(threshold_kernel, "threshold", (field,), [VMEM] * 2)(
+        heat_of_evaporation.reshape(1, BINS), kelvins
+    )[0]
+    partner, threshold = lax.optimization_barrier((partner, threshold))
     facing, inside = call(
         pair_kernel,
         "pair",
-        (shape(BINS + 2, ROWS, WIDTH), shape(BINS + 1, ROWS, WIDTH)),
+        (shape(BINS + 2, *tile), shape(BINS + 1, *tile)),
         [VMEM] * 2,
     )(payload, partner)
-    across = lax.ppermute(facing, "lev", [(0, 3), (3, 0), (1, 2), (2, 1)])
-    condensed, gas = call(phase_kernel, "phase", (field, field), [SMEM] + [VMEM] * 7)(
-        heat_of_evaporation,
+    condensed, gas = call(phase_kernel, "phase", (field, field), [VMEM] * 7)(
         facing,
-        across,
+        lax.ppermute(facing, "lev", cross),
         inside,
         local,
         response,
-        thermal_kelvins,
+        threshold,
         inert_emitted_aerosol,
     )
     return condensed.reshape(bin_burden.shape), gas.reshape(bin_burden.shape)

time: 71.9 us -> 66 us (0.918)
  Pallas kernels: 6.4 us -> 3.45 us
  local copies, waits for them, and re-layouts: 2.95 us -> 0.91 us
  waiting for transfers between devices: 7.25 us -> 6.43 us
    pallas_call x6 -> x9, Pallas kernels: 6.4 us -> 3.45 us  [the longest x1 1.02 us: body(): call(filter_kernel, 'filter', (shape(RING, *tile),), [VMEM] * 5, [pltpu.V...]
    unnamed x22, local copies, waits for them, and re-layouts: 2.95 us -> 0.91 us
  transfers between devices with their start and end apart: 4 -> 4, of which waited for: 3 -> 3; matrix products, arithmetic and copies ran while one was open for 0% -> 0% of each run, Pallas kernels for 0% -> 1%
where the time goes in v2:
time: 66 us; the launch traced here: 65.6 us
  blocking collectives  29.9 us (45%)
  starting transfers between devices  24.1 us (37%)
  waiting for transfers between devices  6.43 us (10%)
  Pallas kernels  3.45 us (5%)
  local copies, waits for them, and re-layouts  0.91 us (1%)
  between operations  0.82 us (1%)
    all_to_all x1, blocking collectives, body(): received = lax.all_to_all(sent, 'lon', 0, 0, tiled=True)  16.5 us
    all_to_all x1, blocking collectives, body(): back = lax.all_to_all(returned, 'lon', 0, 0, tiled=True)  13.4 us
    ppermute x1, starting transfers between devices, body(): lax.ppermute(facing, 'lev', cross)  7.76 us
    ppermute x1, starting transfers between devices, body(): halo_b = lax.ppermute(out_b, 'lat', [(1, 2), (2, 1)])  7.15 us
    ppermute x1, starting transfers between devices, body(): partner = lax.ppermute(payload, 'lev', swap)  6.09 us
    ppermute x1, waiting for transfers between devices, body(): partner = lax.ppermute(payload, 'lev', swap)  3.34 us
    ppermute x1, starting transfers between devices, body(): halo_a = lax.ppermute(out_a, 'lat', swap)  3.11 us
    ppermute x1, waiting for transfers between devices, body(): lax.ppermute(facing, 'lev', cross)  2.01 us
  transfers between devices with their start and end apart: 4, of which 3 were waited for; matrix products, arithmetic and copies ran while one was open for 0% of the time, Pallas kernels for 1%

profile of v2, /device:TPU:4, one launch (start us, length us, event | category | flops | bytes accessed | tf_op | source)
XLA Modules:
  0.0 65.6 jit_solution(15699813386294262977)
XLA Ops:
  0.6 0.0 copy-start
  0.6 0.0 copy-start.1
  0.7 0.0 copy-start.8
  0.7 0.0 copy-start.9
  0.7 0.9 %copy-done = f32[9,4,8,128]{3,2,1,0:T(8,128)S(1)} copy-done((f32[9,4,8,128]{3,2,1,0:T(8,128)S(1)}, f32[9,4,8,128]{3,2,1,0:T(8,128)}, u32[]{:S(2)}) %copy-start) | copy-done | bytes 147480
  1.5 0.0 copy-done.1
  1.5 0.0 copy-done.8
  1.5 0.0 copy-done.9
  1.5 0.0 copy-start.4
  1.6 3.1 %collective-permute-start = (f32[40,1,128]{2,1,0:T(1,128)S(1)}, f32[40,1,128]{2,1,0:T(1,128)S(1)}, u32[]{:S(2)}, u32[]{:S(2)}) collective-permute-start(f32[40,1,128]{2,1,0:T(1,128)S(1)} %get-tuple-element.27), channel_id=1, source_target_pairs={{0,4},{4,0},{8,12},{12,8},{1,5},{5,1},{9,13},{13,9},{2,6},{6,2},{1... | collective-permute-start | bytes 61448 | tf_op jit(solution)/shard_map/ppermute | solution.py:435
  4.7 7.2 %collective-permute-start.1 = (f32[40,1,128]{2,1,0:T(1,128)S(1)}, f32[40,1,128]{2,1,0:T(1,128)S(1)}, u32[]{:S(2)}, u32[]{:S(2)}) collective-permute-start(f32[40,1,128]{2,1,0:T(1,128)S(1)} %get-tuple-element.31), channel_id=1, source_target_pairs={{4,8},{8,4},{5,9},{9,5},{6,10},{10,6},{7,11},{11,7},{20,24},{24,20... | collective-permute-start | bytes 61448 | tf_op jit(solution)/shard_map/ppermute | solution.py:436
  11.9 0.0 copy-done.4
  11.9 0.6 advect.1
  12.5 0.0 collective-permute-done.halo_a
  12.6 1.1 %collective-permute-done.1.halo_b = f32[40,1,128]{2,1,0:T(1,128)S(1)} collective-permute-done((f32[40,1,128]{2,1,0:T(1,128)S(1)}, f32[40,1,128]{2,1,0:T(1,128)S(1)}, u32[]{:S(2)}, u32[]{:S(2)}) %collective-permute-start.1) | collective-permute-done | bytes 20512 | tf_op jit(solution)/shard_map/ppermute | solution.py:436
  13.6 0.2 pack.1
  13.8 0.0 copy-start.2
  13.8 0.0 copy-start.3
  13.8 16.5 %all_to_all.10.received = f32[32,8,128]{2,1,0:T(8,128)S(1)} all-to-all(f32[32,8,128]{2,1,0:T(8,128)S(1)} %get-tuple-element.36), channel_id=1, replica_groups=mesh['lon'=32,'lat'=4,'lev'=4] {'lon'}, dimensions={0} | all-to-all | bytes 262144 | tf_op jit(solution)/shard_map/all_to_all | solution.py:447
  30.3 0.0 copy-done.2
  30.3 0.0 copy-done.3
  30.3 1.0 %filter.1 = f32[32,8,128]{2,1,0:T(8,128)S(1)} custom-call(f32[32,8,128]{2,1,0:T(8,128)S(1)} %all_to_all.10.received, f32[2,8,128]{2,1,0:T(8,128)S(1)} %get-tuple-element.37.packs, f32[2,128,128]{2,1,0:T(8,128)S(1)} %copy-done.2, f32[4,32,128]{2,1,0:T(8,128)S(1)} %copy-done.3, f32[8,128]{1,0:T(8,128)S(1)} %get-tuple-element.38.weight_ref), custom_call_target="tpu_custom_call" | custom-call | flops 10000000 | bytes 100000 | tf_op jit(solution)/shard_map/filter/pallas_call | solution.py:448
  31.3 0.0 copy-start.5
  31.3 13.4 %all_to_all.11.back = f32[32,8,128]{2,1,0:T(8,128)S(1)} all-to-all(f32[32,8,128]{2,1,0:T(8,128)S(1)} %filter.1), channel_id=1, replica_groups=mesh['lon'=32,'lat'=4,'lev'=4] {'lon'}, dimensions={0} | all-to-all | bytes 262144 | tf_op jit(solution)/shard_map/all_to_all | solution.py:455
  44.8 0.0 copy-done.5
  44.8 0.0 copy-start.6
  44.8 0.5 column.1
  45.3 0.0 copy-start.10
  45.3 6.1 %collective-permute-start.2 = (f32[22,8,128]{2,1,0:T(8,128)S(1)}, f32[22,8,128]{2,1,0:T(8,128)S(1)}, u32[]{:S(2)}, u32[]{:S(2)}) collective-permute-start(f32[22,8,128]{2,1,0:T(8,128)S(1)} %get-tuple-element.40.own), channel_id=1, source_target_pairs={{0,1},{1,0},{2,3},{3,2},{4,5},{5,4},{6,7},{7,6},{8,9},{9,8},{10,11... | collective-permute-start | bytes 270344 | tf_op jit(solution)/shard_map/ppermute | solution.py:464
  51.4 0.0 copy-done.6
  51.4 0.0 copy-done.10
  51.4 0.1 threshold.1
  51.5 3.3 %collective-permute-done.2.other = f32[22,8,128]{2,1,0:T(8,128)S(1)} collective-permute-done((f32[22,8,128]{2,1,0:T(8,128)S(1)}, f32[22,8,128]{2,1,0:T(8,128)S(1)}, u32[]{:S(2)}, u32[]{:S(2)}) %collective-permute-start.2) | collective-permute-done | bytes 90144 | tf_op jit(solution)/shard_map/ppermute | solution.py:464
  54.9 0.0 copy-start.7
  54.9 7.8 %collective-permute-start.3 = (f32[11,8,128]{2,1,0:T(8,128)S(1)}, f32[11,8,128]{2,1,0:T(8,128)S(1)}, u32[]{:S(2)}, u32[]{:S(2)}) collective-permute-start(f32[11,8,128]{2,1,0:T(8,128)S(1)} %get-tuple-element.43.own), channel_id=1, source_target_pairs={{0,3},{3,0},{1,2},{2,1},{4,7},{7,4},{5,6},{6,5},{8,11},{11,8},{9,1... | collective-permute-start | bytes 135176 | tf_op jit(solution)/shard_map/ppermute | solution.py:477
  62.7 2.0 %collective-permute-done.3.other = f32[11,8,128]{2,1,0:T(8,128)S(1)} collective-permute-done((f32[11,8,128]{2,1,0:T(8,128)S(1)}, f32[11,8,128]{2,1,0:T(8,128)S(1)}, u32[]{:S(2)}, u32[]{:S(2)}) %collective-permute-start.3) | collective-permute-done | bytes 45088 | tf_op jit(solution)/shard_map/ppermute | solution.py:477
  64.7 0.0 copy-done.7
  64.7 0.9 %phase.1 = (f32[36,8,128]{2,1,0:T(8,128)}, f32[36,8,128]{2,1,0:T(8,128)}) custom-call(f32[11,8,128]{2,1,0:T(8,128)S(1)} %get-tuple-element.43.own, f32[11,8,128]{2,1,0:T(8,128)S(1)} %collective-permute-done.3.other, f32[10,8,128]{2,1,0:T(8,128)S(1)} %get-tuple-element.44.inside, f32[36,8,128]{2,1,0:T(8,128)S(1)} %get-tuple-element.45.local, ...), custom_call_target="tpu_custom_call" | custom-call | flops 10000000 | bytes 100000 | tf_op jit(solution)/shard_map/phase/pallas_call | solution.py:475
  (3 shorter events, 0.1 us)
Async XLA Ops:
  0.6 0.9 %copy-start = (f32[9,4,8,128]{3,2,1,0:T(8,128)S(1)}, f32[9,4,8,128]{3,2,1,0:T(8,128)}, u32[]{:S(2)}) copy-start(f32[9,4,8,128]{3,2,1,0:T(8,128)} %param.11) | copy-start | bytes 442372
  0.6 0.9 %copy-start.1 = (f32[4,8,128]{2,1,0:T(8,128)S(1)}, f32[4,8,128]{2,1,0:T(8,128)}, u32[]{:S(2)}) copy-start(f32[4,8,128]{2,1,0:T(8,128)} %merid.5) | copy-start | bytes 49156
  0.7 0.9 %copy-start.8 = (s32[8]{0:T(128)S(1)}, s32[8]{0:T(128)}, u32[]{:S(2)}) copy-start(s32[8]{0:T(128)} %param.18) | copy-start | bytes 100
  0.7 0.9 %copy-start.9 = (s32[8]{0:T(128)S(1)}, s32[8]{0:T(128)}, u32[]{:S(2)}) copy-start(s32[8]{0:T(128)} %param.19) | copy-start | bytes 100
  1.5 10.3 %copy-start.4 = (f32[4,8,128]{2,1,0:T(8,128)S(1)}, f32[4,8,128]{2,1,0:T(8,128)}, u32[]{:S(2)}) copy-start(f32[4,8,128]{2,1,0:T(8,128)} %zonal.1) | copy-start | bytes 49156
  1.6 10.9 %collective-permute-start = (f32[40,1,128]{2,1,0:T(1,128)S(1)}, f32[40,1,128]{2,1,0:T(1,128)S(1)}, u32[]{:S(2)}, u32[]{:S(2)}) collective-permute-start(f32[40,1,128]{2,1,0:T(1,128)S(1)} %get-tuple-element.27), channel_id=1, source_target_pairs={{0,4},{4,0},{8,12},{12,8},{1,5},{5,1},{9,13},{13,9},{2,6},{6,2},{1... | collective-permute-start | bytes 61448 | tf_op jit(solution)/shard_map/ppermute | solution.py:435
  4.7 8.9 %collective-permute-start.1 = (f32[40,1,128]{2,1,0:T(1,128)S(1)}, f32[40,1,128]{2,1,0:T(1,128)S(1)}, u32[]{:S(2)}, u32[]{:S(2)}) collective-permute-start(f32[40,1,128]{2,1,0:T(1,128)S(1)} %get-tuple-element.31), channel_id=1, source_target_pairs={{4,8},{8,4},{5,9},{9,5},{6,10},{10,6},{7,11},{11,7},{20,24},{24,20... | collective-permute-start | bytes 61448 | tf_op jit(solution)/shard_map/ppermute | solution.py:436
  13.8 16.5 %copy-start.2 = (f32[2,128,128]{2,1,0:T(8,128)S(1)}, f32[2,128,128]{2,1,0:T(8,128)}, u32[]{:S(2)}) copy-start(f32[2,128,128]{2,1,0:T(8,128)} %constant.4.clone.inner) | copy-start | bytes 393220
  13.8 16.5 %copy-start.3 = (f32[4,32,128]{2,1,0:T(8,128)S(1)}, f32[4,32,128]{2,1,0:T(8,128)}, u32[]{:S(2)}) copy-start(f32[4,32,128]{2,1,0:T(8,128)} %constant.5.clone.outer) | copy-start | bytes 196612
  31.3 13.4 %copy-start.5 = (f32[4,8,128]{2,1,0:T(8,128)S(1)}, f32[4,8,128]{2,1,0:T(8,128)}, u32[]{:S(2)}) copy-start(f32[4,8,128]{2,1,0:T(8,128)} %diffusion.1) | copy-start | bytes 49156
  44.8 6.6 %copy-start.6 = (f32[4,8,128]{2,1,0:T(8,128)S(1)}, f32[4,8,128]{2,1,0:T(8,128)}, u32[]{:S(2)}) copy-start(f32[4,8,128]{2,1,0:T(8,128)} %kelvins) | copy-start | bytes 49156
  45.3 6.1 %copy-start.10 = (f32[9]{0:T(128)S(1)}, f32[9]{0:T(128)}, u32[]{:S(2)}) copy-start(f32[9]{0:T(128)} %param.17) | copy-start | bytes 112
  45.3 9.6 %collective-permute-start.2 = (f32[22,8,128]{2,1,0:T(8,128)S(1)}, f32[22,8,128]{2,1,0:T(8,128)S(1)}, u32[]{:S(2)}, u32[]{:S(2)}) collective-permute-start(f32[22,8,128]{2,1,0:T(8,128)S(1)} %get-tuple-element.40.own), channel_id=1, source_target_pairs={{0,1},{1,0},{2,3},{3,2},{4,5},{5,4},{6,7},{7,6},{8,9},{9,8},{10,11... | collective-permute-start | bytes 270344 | tf_op jit(solution)/shard_map/ppermute | solution.py:464
  54.9 9.8 %copy-start.7 = (f32[4,8,128]{2,1,0:T(8,128)S(1)}, f32[4,8,128]{2,1,0:T(8,128)}, u32[]{:S(2)}) copy-start(f32[4,8,128]{2,1,0:T(8,128)} %inert.1) | copy-start | bytes 49156
  54.9 9.8 %collective-permute-start.3 = (f32[11,8,128]{2,1,0:T(8,128)S(1)}, f32[11,8,128]{2,1,0:T(8,128)S(1)}, u32[]{:S(2)}, u32[]{:S(2)}) collective-permute-start(f32[11,8,128]{2,1,0:T(8,128)S(1)} %get-tuple-element.43.own), channel_id=1, source_target_pairs={{0,3},{3,0},{1,2},{2,1},{4,7},{7,4},{5,6},{6,5},{8,11},{11,8},{9,1... | collective-permute-start | bytes 135176 | tf_op jit(solution)/shard_map/ppermute | solution.py:477

commit v3 on v2

--- a/solution.py
+++ b/solution.py
@@ -32,12 +32,12 @@
     return jax.ShapeDtypeStruct(dims, F32)
 
 
-def call(kernel, name, outs, in_specs, scratch=(), flops=10**7):
+def call(kernel, name, outs, in_specs, scratch=(), flops=10**7, place=VMEM):
     return pl.pallas_call(
         kernel,
         out_shape=outs,
         in_specs=in_specs,
-        out_specs=tuple(VMEM for _ in outs),
+        out_specs=tuple(place for _ in outs),
         scratch_shapes=list(scratch),
         compiler_params=pltpu.CompilerParams(vmem_limit_bytes=16 * 2**20),
         cost_estimate=pl.CostEstimate(flops=flops, bytes_accessed=10**5, transcendentals=0),
@@ -200,16 +200,12 @@
     return jnp.where(row == jnp.where(at_south, 0, ROWS - 1), flux, 0.0)
 
 
-def pack_kernel(settings, burden, merid, halo_a, halo_b, partial, faces, bordered, sent):
+def pack_kernel(settings, burden, merid, halo_a, partial, faces, inner, outer, bordered, sent):
     lane, row = iotas()
     odd = lax.axis_index("lat") % 2 == 1
     for t in range(TILES):
         k = t % LEVELS
-        bordered[t] = (
-            partial[t]
-            + border(t, k, odd, row, halo_a, burden, merid)
-            + border(t, k, ~odd, row, halo_b, burden, merid)
-        )
+        bordered[t] = partial[t] + border(t, k, odd, row, halo_a, burden, merid)
     rows = chosen_rows(settings)
     for j in range(RING):
         sent[j, SHARE:, :] = faces[j, SHARE:, :]
@@ -221,57 +217,79 @@
                 sent[j, i : i + 1, :] = jnp.zeros((1, WIDTH), F32)
 
 
+def halves(values):
+    high = values.astype(jnp.bfloat16)
+    return high, (values - high.astype(F32)).astype(jnp.bfloat16)
+
+
+def product(left, right):
+    left_high, left_low = halves(left)
+    right_high, right_low = halves(right)
+
+    def dot(a, b):
+        return jnp.dot(a, b, preferred_element_type=F32)
+
+    return dot(left_high, right_high) + (dot(left_high, right_low) + dot(left_low, right_high))
+
+
 def filter_kernel(received, packs, inner, outer, weight_ref, returned, parts):
     me = lax.axis_index("lon")
-    block = received[...]
-    cosine, sine = inner[0], inner[1]
-    flat = block.reshape(RING * ROWS, WIDTH)
-    parts[...] = jnp.dot(
-        flat,
-        jnp.concatenate([cosine, sine], axis=1),
-        precision=PRECISE,
-        preferred_element_type=F32,
-    )
-    cosine_part = jnp.zeros((ROWS, MODES), F32)
-    sine_part = jnp.zeros((ROWS, MODES), F32)
-    for q in range(RING):
-        c, s = outer[0, q : q + 1, :], outer[1, q : q + 1, :]
-        own_c = parts[ROWS * q : ROWS * (q + 1), :MODES]
-        own_s = parts[ROWS * q : ROWS * (q + 1), MODES:]
-        cosine_part += c * own_c - s * own_s
-        sine_part += s * own_c + c * own_s
-    east_cells = received[:, 5, :]
-    west_cells = received[:, 6, :]
-    faces = received[:, 7, :]
-    beyond = pltpu.roll(east_cells, 1, 0)
-    flux = jnp.maximum(faces, 0.0) * beyond + jnp.minimum(faces, 0.0) * west_cells
-    flux_lane = lax.broadcasted_iota(jnp.int32, flux.shape, 1)
-    flux = jnp.where(flux_lane < SHARE, flux, 0.0)
-    edge = lax.dot_general(
-        flux,
-        jnp.concatenate([outer[2], outer[3]], axis=1),
-        (((0,), (0,)), ((), ())),
-        precision=PRECISE,
-        preferred_element_type=F32,
-    )
-    cosine_part += edge[:ROWS, :MODES]
-    sine_part += edge[:ROWS, MODES:]
-    weight = weight_ref[...]
-    cosine_part *= weight
-    sine_part *= weight
-    for q in range(RING):
-        c, s = outer[0, q : q + 1, :], outer[1, q : q + 1, :]
-        parts[ROWS * q : ROWS * (q + 1), :MODES] = cosine_part * c + sine_part * s
-        parts[ROWS * q : ROWS * (q + 1), MODES:] = sine_part * c - cosine_part * s
-    smooth = jnp.dot(
-        parts[...],
-        jnp.concatenate([cosine, sine], axis=0),
-        precision=PRECISE,
-        preferred_element_type=F32,
-    )
-    returned[...] = smooth.reshape(RING, ROWS, WIDTH)
+    lat = lax.axis_index("lat")
+    active = (lat == 0) | (lat == 3)
+
+    @pl.when(active)
+    def _():
+        block = received[...]
+        cosine, sine = inner[0], inner[1]
+        flat = block.reshape(RING * ROWS, WIDTH)
+        parts[...] = product(flat, jnp.concatenate([cosine, sine], axis=1))
+        cosine_part = jnp.zeros((ROWS, MODES), F32)
+        sine_part = jnp.zeros((ROWS, MODES), F32)
+        for q in range(RING):
+            c, s = outer[0, q : q + 1, :], outer[1, q : q + 1, :]
+            own_c = parts[ROWS * q : ROWS * (q + 1), :MODES]
+            own_s = parts[ROWS * q : ROWS * (q + 1), MODES:]
+            cosine_part += c * own_c - s * own_s
+            sine_part += s * own_c + c * own_s
+        east_cells = received[:, 5, :]
+        west_cells = received[:, 6, :]
+        faces = received[:, 7, :]
+        beyond = pltpu.roll(east_cells, 1, 0)
+        flux = jnp.maximum(faces, 0.0) * beyond + jnp.minimum(faces, 0.0) * west_cells
+        flux_lane = lax.broadcasted_iota(jnp.int32, flux.shape, 1)
+        flux = jnp.where(flux_lane < SHARE, flux, 0.0)
+        edge = lax.dot_general(
+            flux,
+            jnp.concatenate([outer[2], outer[3]], axis=1),
+            (((0,), (0,)), ((), ())),
+            precision=PRECISE,
+            preferred_element_type=F32,
+        )
+        cosine_part += edge[:ROWS, :MODES]
+        sine_part += edge[:ROWS, MODES:]
+        weight = weight_ref[...]
+        cosine_part *= weight
+        sine_part *= weight
+        for q in range(RING):
+            c, s = outer[0, q : q + 1, :], outer[1, q : q + 1, :]
+            parts[ROWS * q : ROWS * (q + 1), :MODES] = cosine_part * c + sine_part * s
+            parts[ROWS * q : ROWS * (q + 1), MODES:] = sine_part * c - cosine_part * s
+        smooth = product(parts[...], jnp.concatenate([cosine, sine], axis=0))
+        returned[...] = smooth.reshape(RING, ROWS, WIDTH)
+
+    @pl.when(jnp.logical_not(active))
+    def _():
+        returned[...] = jnp.zeros((RING, ROWS, WIDTH), F32)
+
     returned[(me + 1) % RING, SHARE:, :] = packs[0, SHARE:, :]
     returned[(me + RING - 1) % RING, SHARE:, :] = packs[1, SHARE:, :]
+
+
+def mend_kernel(burden, merid, halo_b, bordered, mended):
+    lane, row = iotas()
+    even = lax.axis_index("lat") % 2 == 0
+    for t in range(TILES):
+        mended[t] = bordered[t] + border(t, t % LEVELS, even, row, halo_b, burden, merid)
 
 
 def column_kernel(settings, bordered, edges, back, diffusion, local, response, payload):
@@ -374,7 +392,9 @@
         payload[b] = jnp.where(bottom, of_upper(BINS + b), of_lower(b)) + signed * flux
 
 
-def phase_kernel(own, other, inside, local, response, threshold, inert, condensed, gas):
+def phase_kernel(
+    own, other, inside, local, response, threshold, inert, condensed, gas, particles, vapour, sems
+):
     lev = lax.axis_index("lev")
     lower = lev % 2 == 0
     middle = (lev == 1) | (lev == 2)
@@ -387,6 +407,7 @@
         open_end = jnp.where(middle, centre, 0.0)
         below.append(jnp.where(lower, open_end, mid))
         above.append(jnp.where(lower, mid, open_end))
+    copies = []
     for k in range(LEVELS):
         low, up, emitted = response[k], response[LEVELS + k], inert[k]
         totals = [local[b * LEVELS + k] + low * below[b] - up * above[b] for b in range(BINS)]
@@ -399,8 +420,14 @@
             organic = emitted + organic * held
         for b in range(BINS):
             particle = totals[b] * (organic / (organic + limit[b]))
-            condensed[b * LEVELS + k] = particle
-            gas[b * LEVELS + k] = totals[b] - particle
+            particles[b, k] = particle
+            vapour[b, k] = totals[b] - particle
+        for at, (source, target) in enumerate(((particles, condensed), (vapour, gas))):
+            copy = pltpu.make_async_copy(source.at[:, k], target.at[:, k], sems.at[k, at])
+            copy.start()
+            copies.append(copy)
+    for copy in copies:
+        copy.wait()
 
 
 def body(
@@ -442,9 +469,14 @@
     )(settings, burden, zonal_cfl_ratio, meridional_cfl_ratio)
     halo_a, partial, faces = lax.optimization_barrier((halo_a, partial, faces))
     bordered, sent = call(
-        pack_kernel, "pack", (field, shape(RING, *tile)), [VMEM] * 7
-    )(settings, burden, meridional_cfl_ratio, halo_a, halo_b, partial, faces)
+        pack_kernel, "pack", (field, shape(RING, *tile)), [VMEM] * 8
+    )(settings, burden, meridional_cfl_ratio, halo_a, partial, faces, inner, outer)
     received = lax.all_to_all(sent, "lon", 0, 0, tiled=True)
+    received, halo_b = lax.optimization_barrier((received, halo_b))
+    mended = call(mend_kernel, "mend", (field,), [VMEM] * 4)(
+        burden, meridional_cfl_ratio, halo_b, bordered
+    )[0]
+    received, mended = lax.optimization_barrier((received, mended))
     returned = call(
         filter_kernel,
         "filter",
@@ -459,7 +491,7 @@
         "column",
         (field, shape(2 * LEVELS, *tile), shape(count, *tile)),
         [VMEM] * 5,
-    )(settings, bordered, edges, back, diffusion_coefficient)
+    )(settings, mended, edges, back, diffusion_coefficient)
     payload, kelvins = lax.optimization_barrier((payload, thermal_kelvins))
     partner = lax.ppermute(payload, "lev", swap)
     threshold = call(threshold_kernel, "threshold", (field,), [VMEM] * 2)(
@@ -472,7 +504,15 @@
         (shape(BINS + 2, *tile), shape(BINS + 1, *tile)),
         [VMEM] * 2,
     )(payload, partner)
-    condensed, gas = call(phase_kernel, "phase", (field, field), [VMEM] * 7)(
+    result = shape(BINS, LEVELS, *tile)
+    condensed, gas = call(
+        phase_kernel,
+        "phase",
+        (result, result),
+        [VMEM] * 7,
+        [pltpu.VMEM(result.shape, F32)] * 2 + [pltpu.SemaphoreType.DMA((LEVELS, 2))],
+        place=pl.BlockSpec(memory_space=pl.ANY),
+    )(
         facing,
         lax.ppermute(facing, "lev", cross),
         inside,
@@ -481,7 +521,7 @@
         threshold,
         inert_emitted_aerosol,
     )
-    return condensed.reshape(bin_burden.shape), gas.reshape(bin_burden.shape)
+    return condensed, gas
 
 
 def solution(mesh):

time: 66 us -> 63.5 us (0.962)
  the two profiles are of different devices: /device:TPU:4 before, /device:TPU:6 now
where the time goes in v3:
time: 63.5 us; the launch traced here: 63 us
  starting transfers between devices  26.7 us (42%)
  waiting for transfers between devices  17.4 us (27%)
  blocking collectives  13.4 us (21%)
  Pallas kernels  3.8 us (6%)
  local copies, waits for them, and re-layouts  0.91 us (1%)
  between operations  0.82 us (1%)
    all_to_all x1, blocking collectives, body(): back = lax.all_to_all(returned, 'lon', 0, 0, tiled=True)  13.4 us
    all_to_all x1, waiting for transfers between devices, body(): received = lax.all_to_all(sent, 'lon', 0, 0, tiled=True)  9.77 us
    all_to_all x1, starting transfers between devices, body(): received = lax.all_to_all(sent, 'lon', 0, 0, tiled=True)  9.3 us
    ppermute x1, starting transfers between devices, body(): lax.ppermute(facing, 'lev', cross)  7.76 us
    ppermute x1, starting transfers between devices, body(): partner = lax.ppermute(payload, 'lev', swap)  6.09 us
    ppermute x1, waiting for transfers between devices, body(): partner = lax.ppermute(payload, 'lev', swap)  3.34 us
    ppermute x1, starting transfers between devices, body(): halo_a = lax.ppermute(out_a, 'lat', swap)  2.87 us
    ppermute x1, waiting for transfers between devices, body(): halo_a = lax.ppermute(out_a, 'lat', swap)  2.27 us
  transfers between devices with their start and end apart: 5, of which 4 were waited for; matrix products, arithmetic and copies ran while one was open for 0% of the time, Pallas kernels for 1%

profile of v3, /device:TPU:6, one launch (start us, length us, event | category | flops | bytes accessed | tf_op | source)
XLA Modules:
  0.0 63.0 jit_solution(5050866283735272805)
XLA Ops:
  0.6 0.0 copy-start
  0.6 0.0 copy-start.3
  0.7 0.0 copy-start.8
  0.7 0.0 copy-start.9
  0.7 0.9 %copy-done = f32[9,4,8,128]{3,2,1,0:T(8,128)S(1)} copy-done((f32[9,4,8,128]{3,2,1,0:T(8,128)S(1)}, f32[9,4,8,128]{3,2,1,0:T(8,128)}, u32[]{:S(2)}) %copy-start) | copy-done | bytes 147480
  1.5 0.0 copy-done.3
  1.5 0.0 copy-done.8
  1.5 0.0 copy-done.9
  1.5 0.0 copy-start.4
  1.6 0.0 copy-start.2
  1.6 0.0 copy-start.1
  1.6 2.9 %collective-permute-start = (f32[40,1,128]{2,1,0:T(1,128)S(1)}, f32[40,1,128]{2,1,0:T(1,128)S(1)}, u32[]{:S(2)}, u32[]{:S(2)}) collective-permute-start(f32[40,1,128]{2,1,0:T(1,128)S(1)} %get-tuple-element.29), channel_id=1, source_target_pairs={{0,4},{4,0},{8,12},{12,8},{1,5},{5,1},{9,13},{13,9},{2,6},{6,2},{1... | collective-permute-start | bytes 61448 | tf_op jit(solution)/shard_map/ppermute | solution.py:462
  4.5 0.0 copy-done.4
  4.5 0.6 %advect.1 = (f32[36,8,128]{2,1,0:T(8,128)S(1)}, f32[3,8,128]{2,1,0:T(8,128)S(1)}, f32[2,8,128]{2,1,0:T(8,128)S(1)}, f32[32,8,128]{2,1,0:T(8,128)S(1)}, f32[8,128]{1,0:T(8,128)S(1)}) custom-call(s32[8,128]{1,0:T(8,128)S(1)} %get-tuple-element.28.settings, f32[36,8,128]{2,1,0:T(8,128)S(1)} %bitcast.5, f32[4,8,128]{2,1,0:T(8,128)S(1)} %copy-done.4, ...), custom_call_target="tpu_custom_call" | custom-call | flops 10000000 | bytes 100000 | tf_op jit(solution)/shard_map/advect/pallas_call | solution.py:464
  5.2 2.3 %collective-permute-done.halo_a = f32[40,1,128]{2,1,0:T(1,128)S(1)} collective-permute-done((f32[40,1,128]{2,1,0:T(1,128)S(1)}, f32[40,1,128]{2,1,0:T(1,128)S(1)}, u32[]{:S(2)}, u32[]{:S(2)}) %collective-permute-start) | collective-permute-done | bytes 20512 | tf_op jit(solution)/shard_map/ppermute | solution.py:462
  7.4 0.0 copy-done.2
  7.4 0.0 copy-done.1
  7.4 0.8 %pack.1 = (f32[36,8,128]{2,1,0:T(8,128)S(1)}, f32[32,8,128]{2,1,0:T(8,128)}) custom-call(s32[8,128]{1,0:T(8,128)S(1)} %get-tuple-element.28.settings, f32[36,8,128]{2,1,0:T(8,128)S(1)} %bitcast.6, f32[4,8,128]{2,1,0:T(8,128)S(1)} %copy-done.3, f32[40,1,128]{2,1,0:T(1,128)S(1)} %collective-permute-done.halo_a, f32[36,8,128]{2,1,0:T(8,128)S(1)} %get-tuple-element.33.partial, ...), custom_call_target="tpu_custom_call" | custom-call | flops 10000000 | bytes 100000 | tf_op jit(solution)/shard_map/pack/pallas_call | solution.py:471
  8.3 9.3 %all-to-all-start = ((f32[32,8,128]{2,1,0:T(8,128)}), f32[32,8,128]{2,1,0:T(8,128)S(1)}, u32[]{:S(2)}, u32[]{:S(2)}) async-start(f32[32,8,128]{2,1,0:T(8,128)} %get-tuple-element.35), calls=%async_computation | async-start | bytes 262144 | tf_op jit(solution)/shard_map/all_to_all | solution.py:474
  17.6 0.7 %collective-permute-start.1 = (f32[40,1,128]{2,1,0:T(1,128)S(1)}, f32[40,1,128]{2,1,0:T(1,128)S(1)}, u32[]{:S(2)}, u32[]{:S(2)}) collective-permute-start(f32[40,1,128]{2,1,0:T(1,128)S(1)} %get-tuple-element.36), channel_id=1, source_target_pairs={{4,8},{8,4},{5,9},{9,5},{6,10},{10,6},{7,11},{11,7},{20,24},{24,20... | collective-permute-start | bytes 61448 | tf_op jit(solution)/shard_map/ppermute | solution.py:463
  18.2 0.0 collective-permute-done.1.halo_b
  18.3 9.8 %all-to-all-done.received = f32[32,8,128]{2,1,0:T(8,128)S(1)} async-done(((f32[32,8,128]{2,1,0:T(8,128)}), f32[32,8,128]{2,1,0:T(8,128)S(1)}, u32[]{:S(2)}, u32[]{:S(2)}) %all-to-all-start) | async-done | bytes 131104 | tf_op jit(solution)/shard_map/all_to_all | solution.py:474
  28.0 0.1 mend.1.bordered
  28.1 0.7 %filter.1 = f32[32,8,128]{2,1,0:T(8,128)S(1)} custom-call(f32[32,8,128]{2,1,0:T(8,128)S(1)} %all-to-all-done.received, f32[2,8,128]{2,1,0:T(8,128)S(1)} %get-tuple-element.43.packs, f32[2,128,128]{2,1,0:T(8,128)S(1)} %copy-done.1, f32[4,32,128]{2,1,0:T(8,128)S(1)} %copy-done.2, f32[8,128]{1,0:T(8,128)S(1)} %get-tuple-element.44.weight_ref), custom_call_target="tpu_custom_call" | custom-call | flops 10000000 | bytes 100000 | tf_op jit(solution)/shard_map/filter/pallas_call | solution.py:480
  28.8 0.0 copy-start.5
  28.8 13.4 %all_to_all.10.back = f32[32,8,128]{2,1,0:T(8,128)S(1)} all-to-all(f32[32,8,128]{2,1,0:T(8,128)S(1)} %filter.1), channel_id=1, replica_groups=mesh['lon'=32,'lat'=4,'lev'=4] {'lon'}, dimensions={0} | all-to-all | bytes 262144 | tf_op jit(solution)/shard_map/all_to_all | solution.py:487
  42.2 0.0 copy-done.5
  42.2 0.0 copy-start.6
  42.2 0.5 column.1
  42.7 0.0 copy-start.10
  42.8 6.1 %collective-permute-start.2 = (f32[22,8,128]{2,1,0:T(8,128)S(1)}, f32[22,8,128]{2,1,0:T(8,128)S(1)}, u32[]{:S(2)}, u32[]{:S(2)}) collective-permute-start(f32[22,8,128]{2,1,0:T(8,128)S(1)} %get-tuple-element.46.own), channel_id=1, source_target_pairs={{0,1},{1,0},{2,3},{3,2},{4,5},{5,4},{6,7},{7,6},{8,9},{9,8},{10,11... | collective-permute-start | bytes 270344 | tf_op jit(solution)/shard_map/ppermute | solution.py:496
  48.9 0.0 copy-done.6
  48.9 0.0 copy-done.10
  48.9 0.1 threshold.1
  49.0 3.3 %collective-permute-done.2.other = f32[22,8,128]{2,1,0:T(8,128)S(1)} collective-permute-done((f32[22,8,128]{2,1,0:T(8,128)S(1)}, f32[22,8,128]{2,1,0:T(8,128)S(1)}, u32[]{:S(2)}, u32[]{:S(2)}) %collective-permute-start.2) | collective-permute-done | bytes 90144 | tf_op jit(solution)/shard_map/ppermute | solution.py:496
  52.4 0.0 copy-start.7
  52.4 7.8 %collective-permute-start.3 = (f32[11,8,128]{2,1,0:T(8,128)S(1)}, f32[11,8,128]{2,1,0:T(8,128)S(1)}, u32[]{:S(2)}, u32[]{:S(2)}) collective-permute-start(f32[11,8,128]{2,1,0:T(8,128)S(1)} %get-tuple-element.49.own), channel_id=1, source_target_pairs={{0,3},{3,0},{1,2},{2,1},{4,7},{7,4},{5,6},{6,5},{8,11},{11,8},{9,1... | collective-permute-start | bytes 135176 | tf_op jit(solution)/shard_map/ppermute | solution.py:517
  60.2 2.0 %collective-permute-done.3.other = f32[11,8,128]{2,1,0:T(8,128)S(1)} collective-permute-done((f32[11,8,128]{2,1,0:T(8,128)S(1)}, f32[11,8,128]{2,1,0:T(8,128)S(1)}, u32[]{:S(2)}, u32[]{:S(2)}) %collective-permute-start.3) | collective-permute-done | bytes 45088 | tf_op jit(solution)/shard_map/ppermute | solution.py:517
  62.2 0.0 copy-done.7
  62.2 0.9 %phase.1 = (f32[9,4,8,128]{3,2,1,0:T(8,128)}, f32[9,4,8,128]{3,2,1,0:T(8,128)}) custom-call(f32[11,8,128]{2,1,0:T(8,128)S(1)} %get-tuple-element.49.own, f32[11,8,128]{2,1,0:T(8,128)S(1)} %collective-permute-done.3.other, f32[10,8,128]{2,1,0:T(8,128)S(1)} %get-tuple-element.50.inside, f32[36,8,128]{2,1,0:T(8,128)S(1)} %get-tuple-element.51.local, ...), custom_call_target="tpu_custom_call" | custom-call | flops 10000000 | bytes 100000 | tf_op jit(solution)/shard_map/phase/pallas_call | solution.py:508
  (3 shorter events, 0.1 us)
Async XLA Ops:
  0.6 0.9 %copy-start = (f32[9,4,8,128]{3,2,1,0:T(8,128)S(1)}, f32[9,4,8,128]{3,2,1,0:T(8,128)}, u32[]{:S(2)}) copy-start(f32[9,4,8,128]{3,2,1,0:T(8,128)} %param.11) | copy-start | bytes 442372
  0.6 0.9 %copy-start.3 = (f32[4,8,128]{2,1,0:T(8,128)S(1)}, f32[4,8,128]{2,1,0:T(8,128)}, u32[]{:S(2)}) copy-start(f32[4,8,128]{2,1,0:T(8,128)} %merid.7) | copy-start | bytes 49156
  0.7 0.9 %copy-start.8 = (s32[8]{0:T(128)S(1)}, s32[8]{0:T(128)}, u32[]{:S(2)}) copy-start(s32[8]{0:T(128)} %param.18) | copy-start | bytes 100
  0.7 0.9 %copy-start.9 = (s32[8]{0:T(128)S(1)}, s32[8]{0:T(128)}, u32[]{:S(2)}) copy-start(s32[8]{0:T(128)} %param.19) | copy-start | bytes 100
  1.5 3.0 %copy-start.4 = (f32[4,8,128]{2,1,0:T(8,128)S(1)}, f32[4,8,128]{2,1,0:T(8,128)}, u32[]{:S(2)}) copy-start(f32[4,8,128]{2,1,0:T(8,128)} %zonal.1) | copy-start | bytes 49156
  1.6 5.9 %copy-start.2 = (f32[4,32,128]{2,1,0:T(8,128)S(1)}, f32[4,32,128]{2,1,0:T(8,128)}, u32[]{:S(2)}) copy-start(f32[4,32,128]{2,1,0:T(8,128)} %constant.5.clone.outer) | copy-start | bytes 196612
  1.6 5.8 %copy-start.1 = (f32[2,128,128]{2,1,0:T(8,128)S(1)}, f32[2,128,128]{2,1,0:T(8,128)}, u32[]{:S(2)}) copy-start(f32[2,128,128]{2,1,0:T(8,128)} %constant.4.clone.inner) | copy-start | bytes 393220
  1.6 5.8 %collective-permute-start = (f32[40,1,128]{2,1,0:T(1,128)S(1)}, f32[40,1,128]{2,1,0:T(1,128)S(1)}, u32[]{:S(2)}, u32[]{:S(2)}) collective-permute-start(f32[40,1,128]{2,1,0:T(1,128)S(1)} %get-tuple-element.29), channel_id=1, source_target_pairs={{0,4},{4,0},{8,12},{12,8},{1,5},{5,1},{9,13},{13,9},{2,6},{6,2},{1... | collective-permute-start | bytes 61448 | tf_op jit(solution)/shard_map/ppermute | solution.py:462
  8.3 19.8 %all-to-all-start = ((f32[32,8,128]{2,1,0:T(8,128)}), f32[32,8,128]{2,1,0:T(8,128)S(1)}, u32[]{:S(2)}, u32[]{:S(2)}) async-start(f32[32,8,128]{2,1,0:T(8,128)} %get-tuple-element.35), calls=%async_computation | async-start | bytes 262144 | tf_op jit(solution)/shard_map/all_to_all | solution.py:474
  17.6 0.7 %collective-permute-start.1 = (f32[40,1,128]{2,1,0:T(1,128)S(1)}, f32[40,1,128]{2,1,0:T(1,128)S(1)}, u32[]{:S(2)}, u32[]{:S(2)}) collective-permute-start(f32[40,1,128]{2,1,0:T(1,128)S(1)} %get-tuple-element.36), channel_id=1, source_target_pairs={{4,8},{8,4},{5,9},{9,5},{6,10},{10,6},{7,11},{11,7},{20,24},{24,20... | collective-permute-start | bytes 61448 | tf_op jit(solution)/shard_map/ppermute | solution.py:463
  28.8 13.4 %copy-start.5 = (f32[4,8,128]{2,1,0:T(8,128)S(1)}, f32[4,8,128]{2,1,0:T(8,128)}, u32[]{:S(2)}) copy-start(f32[4,8,128]{2,1,0:T(8,128)} %diffusion.1) | copy-start | bytes 49156
  42.2 6.6 %copy-start.6 = (f32[4,8,128]{2,1,0:T(8,128)S(1)}, f32[4,8,128]{2,1,0:T(8,128)}, u32[]{:S(2)}) copy-start(f32[4,8,128]{2,1,0:T(8,128)} %kelvins) | copy-start | bytes 49156
  42.7 6.1 %copy-start.10 = (f32[9]{0:T(128)S(1)}, f32[9]{0:T(128)}, u32[]{:S(2)}) copy-start(f32[9]{0:T(128)} %param.17) | copy-start | bytes 112
  42.8 9.6 %collective-permute-start.2 = (f32[22,8,128]{2,1,0:T(8,128)S(1)}, f32[22,8,128]{2,1,0:T(8,128)S(1)}, u32[]{:S(2)}, u32[]{:S(2)}) collective-permute-start(f32[22,8,128]{2,1,0:T(8,128)S(1)} %get-tuple-element.46.own), channel_id=1, source_target_pairs={{0,1},{1,0},{2,3},{3,2},{4,5},{5,4},{6,7},{7,6},{8,9},{9,8},{10,11... | collective-permute-start | bytes 270344 | tf_op jit(solution)/shard_map/ppermute | solution.py:496
  52.4 9.8 %copy-start.7 = (f32[4,8,128]{2,1,0:T(8,128)S(1)}, f32[4,8,128]{2,1,0:T(8,128)}, u32[]{:S(2)}) copy-start(f32[4,8,128]{2,1,0:T(8,128)} %inert.1) | copy-start | bytes 49156
  52.4 9.8 %collective-permute-start.3 = (f32[11,8,128]{2,1,0:T(8,128)S(1)}, f32[11,8,128]{2,1,0:T(8,128)S(1)}, u32[]{:S(2)}, u32[]{:S(2)}) collective-permute-start(f32[11,8,128]{2,1,0:T(8,128)S(1)} %get-tuple-element.49.own), channel_id=1, source_target_pairs={{0,3},{3,0},{1,2},{2,1},{4,7},{7,4},{5,6},{6,5},{8,11},{11,8},{9,1... | collective-permute-start | bytes 135176 | tf_op jit(solution)/shard_map/ppermute | solution.py:517

commit v4 on v3

--- a/solution.py
+++ b/solution.py
@@ -285,32 +285,11 @@
     returned[(me + RING - 1) % RING, SHARE:, :] = packs[1, SHARE:, :]
 
 
-def mend_kernel(burden, merid, halo_b, bordered, mended):
+def mend_kernel(burden, merid, halo_b, bordered, diffusion, mended, response, factors):
     lane, row = iotas()
     even = lax.axis_index("lat") % 2 == 0
     for t in range(TILES):
         mended[t] = bordered[t] + border(t, t % LEVELS, even, row, halo_b, burden, merid)
-
-
-def column_kernel(settings, bordered, edges, back, diffusion, local, response, payload):
-    lane, row = iotas()
-    me = lax.axis_index("lon")
-    east_own, west_own, face_own = edges[0], edges[1], edges[2]
-    from_west = unsqueeze_rows(back[(me + RING - 1) % RING], row)
-    from_east = unsqueeze_rows(back[(me + 1) % RING], row)
-    four = jnp.where(lane < LEVELS, pltpu.roll(from_east, WIDTH - TILES, 1), 0.0)
-    eight = four + pltpu.roll(four, 4, 1)
-    sixteen = eight + pltpu.roll(eight, 8, 1)
-    face_next = sixteen + pltpu.roll(sixteen, 16, 1) + pltpu.roll(four, 32, 1)
-    flux_in = jnp.maximum(face_own, 0.0) * from_west + jnp.minimum(face_own, 0.0) * west_own
-    flux_out = jnp.maximum(face_next, 0.0) * east_own + jnp.minimum(face_next, 0.0) * from_east
-    lat = lax.axis_index("lat")
-    active = (lat == 0) | (lat == 3)
-    here = []
-    for p in range(POLE):
-        north, south = settings[0:1, p : p + 1], settings[0:1, POLE + p : POLE + p + 1] - 3 * ROWS
-        chosen = jnp.broadcast_to(jnp.where(lat == 0, north, south), (ROWS, WIDTH))
-        here.append((row == chosen) & active)
     a1, a2, a3 = diffusion[1], diffusion[2], diffusion[3]
     i0 = 1.0 / (1.0 + a1)
     w1 = a1 * i0
@@ -332,6 +311,31 @@
     low0 = i0 + w1 * low1
     for at, value in enumerate((low0, low1, low2, low3, up0, up1, up2, up3)):
         response[at] = value
+    for at, value in enumerate((i0, i1, i2, i3, w1, w2, w3, low0 + 1.0 / diffusion[0])):
+        factors[at] = value
+
+
+def column_kernel(settings, bordered, edges, back, response, factors, local, payload):
+    lane, row = iotas()
+    me = lax.axis_index("lon")
+    east_own, west_own, face_own = edges[0], edges[1], edges[2]
+    from_west = unsqueeze_rows(back[(me + RING - 1) % RING], row)
+    from_east = unsqueeze_rows(back[(me + 1) % RING], row)
+    four = jnp.where(lane < LEVELS, pltpu.roll(from_east, WIDTH - TILES, 1), 0.0)
+    eight = four + pltpu.roll(four, 4, 1)
+    sixteen = eight + pltpu.roll(eight, 8, 1)
+    face_next = sixteen + pltpu.roll(sixteen, 16, 1) + pltpu.roll(four, 32, 1)
+    flux_in = jnp.maximum(face_own, 0.0) * from_west + jnp.minimum(face_own, 0.0) * west_own
+    flux_out = jnp.maximum(face_next, 0.0) * east_own + jnp.minimum(face_next, 0.0) * from_east
+    lat = lax.axis_index("lat")
+    active = (lat == 0) | (lat == 3)
+    here = []
+    for p in range(POLE):
+        north, south = settings[0:1, p : p + 1], settings[0:1, POLE + p : POLE + p + 1] - 3 * ROWS
+        chosen = jnp.broadcast_to(jnp.where(lat == 0, north, south), (ROWS, WIDTH))
+        here.append((row == chosen) & active)
+    i0, i1, i2, i3 = (factors[at] for at in range(4))
+    w1, w2, w3 = (factors[at] for at in range(4, 7))
     for b in range(BINS):
         source = []
         for k in range(LEVELS):
@@ -360,10 +364,9 @@
         local[b * LEVELS + 3] = x3
         payload[b] = x0
         payload[BINS + b] = x3
-    payload[2 * BINS] = low0
-    payload[2 * BINS + 1] = up3
-    payload[2 * BINS + 2] = up0
-    payload[2 * BINS + 3] = 1.0 / diffusion[0]
+    payload[2 * BINS] = factors[7]
+    payload[2 * BINS + 1] = response[2 * LEVELS - 1]
+    payload[2 * BINS + 2] = response[LEVELS]
 
 
 def pair_kernel(own, other, payload, inside):
@@ -377,7 +380,7 @@
     def of_upper(at):
         return jnp.where(lower, other[at], own[at])
 
-    scale = 1.0 / (of_upper(2 * BINS + 3) + of_lower(2 * BINS + 1) + of_upper(2 * BINS))
+    scale = 1.0 / (of_lower(2 * BINS + 1) + of_upper(2 * BINS))
     through = jnp.where(bottom, of_upper(2 * BINS + 2), of_lower(2 * BINS + 2))
     coupling = through * scale
     facing = jnp.where(bottom, of_upper(2 * BINS + 1), of_lower(2 * BINS))
@@ -385,7 +388,6 @@
     signed = through * sign
     inside[BINS] = coupling
     payload[BINS] = facing - through * coupling
-    payload[BINS + 1] = jnp.where(bottom, 0.0, of_lower(2 * BINS + 3))
     for b in range(BINS):
         flux = (of_lower(BINS + b) - of_upper(b)) * scale
         inside[b] = flux
@@ -399,7 +401,7 @@
     lower = lev % 2 == 0
     middle = (lev == 1) | (lev == 2)
     sign = jnp.where(lev < 2, 1.0, -1.0)
-    scale = sign / (own[BINS + 1] + other[BINS + 1] + own[BINS] + other[BINS])
+    scale = sign / (own[BINS] + other[BINS])
     below, above = [], []
     for b in range(BINS):
         centre = (own[b] - other[b]) * scale
@@ -473,9 +475,10 @@
     )(settings, burden, meridional_cfl_ratio, halo_a, partial, faces, inner, outer)
     received = lax.all_to_all(sent, "lon", 0, 0, tiled=True)
     received, halo_b = lax.optimization_barrier((received, halo_b))
-    mended = call(mend_kernel, "mend", (field,), [VMEM] * 4)(
-        burden, meridional_cfl_ratio, halo_b, bordered
-    )[0]
+    eight = shape(2 * LEVELS, *tile)
+    mended, response, factors = call(mend_kernel, "mend", (field, eight, eight), [VMEM] * 5)(
+        burden, meridional_cfl_ratio, halo_b, bordered, diffusion_coefficient
+    )
     received, mended = lax.optimization_barrier((received, mended))
     returned = call(
         filter_kernel,
@@ -485,13 +488,9 @@
         [pltpu.VMEM((RING * ROWS, 2 * MODES), F32)],
     )(received, packs, inner, outer, weight)[0]
     back = lax.all_to_all(returned, "lon", 0, 0, tiled=True)
-    count = 2 * BINS + 4
-    local, response, payload = call(
-        column_kernel,
-        "column",
-        (field, shape(2 * LEVELS, *tile), shape(count, *tile)),
-        [VMEM] * 5,
-    )(settings, mended, edges, back, diffusion_coefficient)
+    local, payload = call(
+        column_kernel, "column", (field, shape(2 * BINS + 3, *tile)), [VMEM] * 6
+    )(settings, mended, edges, back, response, factors)
     payload, kelvins = lax.optimization_barrier((payload, thermal_kelvins))
     partner = lax.ppermute(payload, "lev", swap)
     threshold = call(threshold_kernel, "threshold", (field,), [VMEM] * 2)(
@@ -501,7 +500,7 @@
     facing, inside = call(
         pair_kernel,
         "pair",
-        (shape(BINS + 2, *tile), shape(BINS + 1, *tile)),
+        (shape(BINS + 1, *tile), shape(BINS + 1, *tile)),
         [VMEM] * 2,
     )(payload, partner)
     result = shape(BINS, LEVELS, *tile)

time: 63.5 us -> 63.5 us (level)
  no operation moved by 1% of the time
where the time goes in v4:
time: 63.5 us; the launch traced here: 63.1 us
  starting transfers between devices  26.9 us (42%)
  waiting for transfers between devices  17.2 us (27%)
  blocking collectives  13.4 us (21%)
  Pallas kernels  3.83 us (6%)
  local copies, waits for them, and re-layouts  0.91 us (1%)
  between operations  0.82 us (1%)
    all_to_all x1, blocking collectives, body(): back = lax.all_to_all(returned, 'lon', 0, 0, tiled=True)  13.4 us
    all_to_all x1, waiting for transfers between devices, body(): received = lax.all_to_all(sent, 'lon', 0, 0, tiled=True)  9.77 us
    all_to_all x1, starting transfers between devices, body(): received = lax.all_to_all(sent, 'lon', 0, 0, tiled=True)  9.43 us
    ppermute x1, starting transfers between devices, body(): lax.ppermute(facing, 'lev', cross)  7.9 us
    ppermute x1, starting transfers between devices, body(): partner = lax.ppermute(payload, 'lev', swap)  6.09 us
    ppermute x1, waiting for transfers between devices, body(): partner = lax.ppermute(payload, 'lev', swap)  3.16 us
    ppermute x1, starting transfers between devices, body(): halo_a = lax.ppermute(out_a, 'lat', swap)  2.87 us
    ppermute x1, waiting for transfers between devices, body(): halo_a = lax.ppermute(out_a, 'lat', swap)  2.27 us
  transfers between devices with their start and end apart: 5, of which 4 were waited for; matrix products, arithmetic and copies ran while one was open for 0% of the time, Pallas kernels for 1%

profile of v4, /device:TPU:6, one launch (start us, length us, event | category | flops | bytes accessed | tf_op | source)
XLA Modules:
  0.0 63.1 jit_solution(15472182728287282639)
XLA Ops:
  0.6 0.0 copy-start
  0.6 0.0 copy-start.3
  0.7 0.0 copy-start.8
  0.7 0.0 copy-start.9
  0.7 0.9 %copy-done = f32[9,4,8,128]{3,2,1,0:T(8,128)S(1)} copy-done((f32[9,4,8,128]{3,2,1,0:T(8,128)S(1)}, f32[9,4,8,128]{3,2,1,0:T(8,128)}, u32[]{:S(2)}) %copy-start) | copy-done | bytes 147480
  1.5 0.0 copy-done.3
  1.5 0.0 copy-done.8
  1.5 0.0 copy-done.9
  1.5 0.0 copy-start.4
  1.6 0.0 copy-start.2
  1.6 0.0 copy-start.1
  1.6 2.9 %collective-permute-start = (f32[40,1,128]{2,1,0:T(1,128)S(1)}, f32[40,1,128]{2,1,0:T(1,128)S(1)}, u32[]{:S(2)}, u32[]{:S(2)}) collective-permute-start(f32[40,1,128]{2,1,0:T(1,128)S(1)} %get-tuple-element.31), channel_id=1, source_target_pairs={{0,4},{4,0},{8,12},{12,8},{1,5},{5,1},{9,13},{13,9},{2,6},{6,2},{1... | collective-permute-start | bytes 61448 | tf_op jit(solution)/shard_map/ppermute | solution.py:464
  4.5 0.0 copy-done.4
  4.5 0.6 %advect.1 = (f32[36,8,128]{2,1,0:T(8,128)S(1)}, f32[3,8,128]{2,1,0:T(8,128)S(1)}, f32[2,8,128]{2,1,0:T(8,128)S(1)}, f32[32,8,128]{2,1,0:T(8,128)S(1)}, f32[8,128]{1,0:T(8,128)S(1)}) custom-call(s32[8,128]{1,0:T(8,128)S(1)} %get-tuple-element.30.settings, f32[36,8,128]{2,1,0:T(8,128)S(1)} %bitcast.5, f32[4,8,128]{2,1,0:T(8,128)S(1)} %copy-done.4, ...), custom_call_target="tpu_custom_call" | custom-call | flops 10000000 | bytes 100000 | tf_op jit(solution)/shard_map/advect/pallas_call | solution.py:466
  5.2 2.3 %collective-permute-done.halo_a = f32[40,1,128]{2,1,0:T(1,128)S(1)} collective-permute-done((f32[40,1,128]{2,1,0:T(1,128)S(1)}, f32[40,1,128]{2,1,0:T(1,128)S(1)}, u32[]{:S(2)}, u32[]{:S(2)}) %collective-permute-start) | collective-permute-done | bytes 20512 | tf_op jit(solution)/shard_map/ppermute | solution.py:464
  7.4 0.0 copy-done.2
  7.4 0.0 copy-done.1
  7.4 0.8 %pack.1 = (f32[36,8,128]{2,1,0:T(8,128)S(1)}, f32[32,8,128]{2,1,0:T(8,128)}) custom-call(s32[8,128]{1,0:T(8,128)S(1)} %get-tuple-element.30.settings, f32[36,8,128]{2,1,0:T(8,128)S(1)} %bitcast.6, f32[4,8,128]{2,1,0:T(8,128)S(1)} %copy-done.3, f32[40,1,128]{2,1,0:T(1,128)S(1)} %collective-permute-done.halo_a, f32[36,8,128]{2,1,0:T(8,128)S(1)} %get-tuple-element.35.partial, ...), custom_call_target="tpu_custom_call" | custom-call | flops 10000000 | bytes 100000 | tf_op jit(solution)/shard_map/pack/pallas_call | solution.py:473
  8.3 0.0 copy-start.5
  8.3 9.4 %all-to-all-start = ((f32[32,8,128]{2,1,0:T(8,128)}), f32[32,8,128]{2,1,0:T(8,128)S(1)}, u32[]{:S(2)}, u32[]{:S(2)}) async-start(f32[32,8,128]{2,1,0:T(8,128)} %get-tuple-element.37), calls=%async_computation | async-start | bytes 262144 | tf_op jit(solution)/shard_map/all_to_all | solution.py:476
  17.7 0.7 %collective-permute-start.1 = (f32[40,1,128]{2,1,0:T(1,128)S(1)}, f32[40,1,128]{2,1,0:T(1,128)S(1)}, u32[]{:S(2)}, u32[]{:S(2)}) collective-permute-start(f32[40,1,128]{2,1,0:T(1,128)S(1)} %get-tuple-element.38), channel_id=1, source_target_pairs={{4,8},{8,4},{5,9},{9,5},{6,10},{10,6},{7,11},{11,7},{20,24},{24,20... | collective-permute-start | bytes 61448 | tf_op jit(solution)/shard_map/ppermute | solution.py:465
  18.4 0.0 collective-permute-done.1.halo_b
  18.4 9.8 %all-to-all-done.received = f32[32,8,128]{2,1,0:T(8,128)S(1)} async-done(((f32[32,8,128]{2,1,0:T(8,128)}), f32[32,8,128]{2,1,0:T(8,128)S(1)}, u32[]{:S(2)}, u32[]{:S(2)}) %all-to-all-start) | async-done | bytes 131104 | tf_op jit(solution)/shard_map/all_to_all | solution.py:476
  28.2 0.0 copy-done.5
  28.2 0.1 mend.1
  28.3 0.7 %filter.1 = f32[32,8,128]{2,1,0:T(8,128)S(1)} custom-call(f32[32,8,128]{2,1,0:T(8,128)S(1)} %all-to-all-done.received, f32[2,8,128]{2,1,0:T(8,128)S(1)} %get-tuple-element.46.packs, f32[2,128,128]{2,1,0:T(8,128)S(1)} %copy-done.1, f32[4,32,128]{2,1,0:T(8,128)S(1)} %copy-done.2, f32[8,128]{1,0:T(8,128)S(1)} %get-tuple-element.47.weight_ref), custom_call_target="tpu_custom_call" | custom-call | flops 10000000 | bytes 100000 | tf_op jit(solution)/shard_map/filter/pallas_call | solution.py:483
  29.0 13.4 %all_to_all.10.back = f32[32,8,128]{2,1,0:T(8,128)S(1)} all-to-all(f32[32,8,128]{2,1,0:T(8,128)S(1)} %filter.1), channel_id=1, replica_groups=mesh['lon'=32,'lat'=4,'lev'=4] {'lon'}, dimensions={0} | all-to-all | bytes 262144 | tf_op jit(solution)/shard_map/all_to_all | solution.py:490
  42.4 0.0 copy-start.6
  42.4 0.5 column.1
  42.9 0.0 copy-start.10
  42.9 6.1 %collective-permute-start.2 = (f32[21,8,128]{2,1,0:T(8,128)S(1)}, f32[21,8,128]{2,1,0:T(8,128)S(1)}, u32[]{:S(2)}, u32[]{:S(2)}) collective-permute-start(f32[21,8,128]{2,1,0:T(8,128)S(1)} %get-tuple-element.51.own), channel_id=1, source_target_pairs={{0,1},{1,0},{2,3},{3,2},{4,5},{5,4},{6,7},{7,6},{8,9},{9,8},{10,11... | collective-permute-start | bytes 258056 | tf_op jit(solution)/shard_map/ppermute | solution.py:495
  49.0 0.0 copy-done.6
  49.0 0.0 copy-done.10
  49.0 0.0 copy-start.7
  49.0 0.1 threshold.1
  49.2 3.2 %collective-permute-done.2.other = f32[21,8,128]{2,1,0:T(8,128)S(1)} collective-permute-done((f32[21,8,128]{2,1,0:T(8,128)S(1)}, f32[21,8,128]{2,1,0:T(8,128)S(1)}, u32[]{:S(2)}, u32[]{:S(2)}) %collective-permute-start.2) | collective-permute-done | bytes 86048 | tf_op jit(solution)/shard_map/ppermute | solution.py:495
  52.4 7.9 %collective-permute-start.3 = (f32[10,8,128]{2,1,0:T(8,128)S(1)}, f32[10,8,128]{2,1,0:T(8,128)S(1)}, u32[]{:S(2)}, u32[]{:S(2)}) collective-permute-start(f32[10,8,128]{2,1,0:T(8,128)S(1)} %get-tuple-element.54.own), channel_id=1, source_target_pairs={{0,3},{3,0},{1,2},{2,1},{4,7},{7,4},{5,6},{6,5},{8,11},{11,8},{9,1... | collective-permute-start | bytes 122888 | tf_op jit(solution)/shard_map/ppermute | solution.py:516
  60.3 2.0 %collective-permute-done.3.other = f32[10,8,128]{2,1,0:T(8,128)S(1)} collective-permute-done((f32[10,8,128]{2,1,0:T(8,128)S(1)}, f32[10,8,128]{2,1,0:T(8,128)S(1)}, u32[]{:S(2)}, u32[]{:S(2)}) %collective-permute-start.3) | collective-permute-done | bytes 40992 | tf_op jit(solution)/shard_map/ppermute | solution.py:516
  62.2 0.0 copy-done.7
  62.2 0.9 %phase.1 = (f32[9,4,8,128]{3,2,1,0:T(8,128)}, f32[9,4,8,128]{3,2,1,0:T(8,128)}) custom-call(f32[10,8,128]{2,1,0:T(8,128)S(1)} %get-tuple-element.54.own, f32[10,8,128]{2,1,0:T(8,128)S(1)} %collective-permute-done.3.other, f32[10,8,128]{2,1,0:T(8,128)S(1)} %get-tuple-element.55.inside, f32[36,8,128]{2,1,0:T(8,128)S(1)} %get-tuple-element.56.local, ...), custom_call_target="tpu_custom_call" | custom-call | flops 10000000 | bytes 100000 | tf_op jit(solution)/shard_map/phase/pallas_call | solution.py:507
  (3 shorter events, 0.1 us)
Async XLA Ops:
  0.6 0.9 %copy-start = (f32[9,4,8,128]{3,2,1,0:T(8,128)S(1)}, f32[9,4,8,128]{3,2,1,0:T(8,128)}, u32[]{:S(2)}) copy-start(f32[9,4,8,128]{3,2,1,0:T(8,128)} %param.11) | copy-start | bytes 442372
  0.6 0.9 %copy-start.3 = (f32[4,8,128]{2,1,0:T(8,128)S(1)}, f32[4,8,128]{2,1,0:T(8,128)}, u32[]{:S(2)}) copy-start(f32[4,8,128]{2,1,0:T(8,128)} %merid.7) | copy-start | bytes 49156
  0.7 0.9 %copy-start.8 = (s32[8]{0:T(128)S(1)}, s32[8]{0:T(128)}, u32[]{:S(2)}) copy-start(s32[8]{0:T(128)} %param.18) | copy-start | bytes 100
  0.7 0.9 %copy-start.9 = (s32[8]{0:T(128)S(1)}, s32[8]{0:T(128)}, u32[]{:S(2)}) copy-start(s32[8]{0:T(128)} %param.19) | copy-start | bytes 100
  1.5 3.0 %copy-start.4 = (f32[4,8,128]{2,1,0:T(8,128)S(1)}, f32[4,8,128]{2,1,0:T(8,128)}, u32[]{:S(2)}) copy-start(f32[4,8,128]{2,1,0:T(8,128)} %zonal.1) | copy-start | bytes 49156
  1.6 5.9 %copy-start.2 = (f32[4,32,128]{2,1,0:T(8,128)S(1)}, f32[4,32,128]{2,1,0:T(8,128)}, u32[]{:S(2)}) copy-start(f32[4,32,128]{2,1,0:T(8,128)} %constant.5.clone.outer) | copy-start | bytes 196612
  1.6 5.8 %copy-start.1 = (f32[2,128,128]{2,1,0:T(8,128)S(1)}, f32[2,128,128]{2,1,0:T(8,128)}, u32[]{:S(2)}) copy-start(f32[2,128,128]{2,1,0:T(8,128)} %constant.4.clone.inner) | copy-start | bytes 393220
  1.6 5.8 %collective-permute-start = (f32[40,1,128]{2,1,0:T(1,128)S(1)}, f32[40,1,128]{2,1,0:T(1,128)S(1)}, u32[]{:S(2)}, u32[]{:S(2)}) collective-permute-start(f32[40,1,128]{2,1,0:T(1,128)S(1)} %get-tuple-element.31), channel_id=1, source_target_pairs={{0,4},{4,0},{8,12},{12,8},{1,5},{5,1},{9,13},{13,9},{2,6},{6,2},{1... | collective-permute-start | bytes 61448 | tf_op jit(solution)/shard_map/ppermute | solution.py:464
  8.3 19.9 %copy-start.5 = (f32[4,8,128]{2,1,0:T(8,128)S(1)}, f32[4,8,128]{2,1,0:T(8,128)}, u32[]{:S(2)}) copy-start(f32[4,8,128]{2,1,0:T(8,128)} %diffusion.1) | copy-start | bytes 49156
  8.3 19.9 %all-to-all-start = ((f32[32,8,128]{2,1,0:T(8,128)}), f32[32,8,128]{2,1,0:T(8,128)S(1)}, u32[]{:S(2)}, u32[]{:S(2)}) async-start(f32[32,8,128]{2,1,0:T(8,128)} %get-tuple-element.37), calls=%async_computation | async-start | bytes 262144 | tf_op jit(solution)/shard_map/all_to_all | solution.py:476
  17.7 0.7 %collective-permute-start.1 = (f32[40,1,128]{2,1,0:T(1,128)S(1)}, f32[40,1,128]{2,1,0:T(1,128)S(1)}, u32[]{:S(2)}, u32[]{:S(2)}) collective-permute-start(f32[40,1,128]{2,1,0:T(1,128)S(1)} %get-tuple-element.38), channel_id=1, source_target_pairs={{4,8},{8,4},{5,9},{9,5},{6,10},{10,6},{7,11},{11,7},{20,24},{24,20... | collective-permute-start | bytes 61448 | tf_op jit(solution)/shard_map/ppermute | solution.py:465
  42.4 6.6 %copy-start.6 = (f32[4,8,128]{2,1,0:T(8,128)S(1)}, f32[4,8,128]{2,1,0:T(8,128)}, u32[]{:S(2)}) copy-start(f32[4,8,128]{2,1,0:T(8,128)} %kelvins) | copy-start | bytes 49156
  42.9 6.1 %copy-start.10 = (f32[9]{0:T(128)S(1)}, f32[9]{0:T(128)}, u32[]{:S(2)}) copy-start(f32[9]{0:T(128)} %param.17) | copy-start | bytes 112
  42.9 9.4 %collective-permute-start.2 = (f32[21,8,128]{2,1,0:T(8,128)S(1)}, f32[21,8,128]{2,1,0:T(8,128)S(1)}, u32[]{:S(2)}, u32[]{:S(2)}) collective-permute-start(f32[21,8,128]{2,1,0:T(8,128)S(1)} %get-tuple-element.51.own), channel_id=1, source_target_pairs={{0,1},{1,0},{2,3},{3,2},{4,5},{5,4},{6,7},{7,6},{8,9},{9,8},{10,11... | collective-permute-start | bytes 258056 | tf_op jit(solution)/shard_map/ppermute | solution.py:495
  49.0 13.2 %copy-start.7 = (f32[4,8,128]{2,1,0:T(8,128)S(1)}, f32[4,8,128]{2,1,0:T(8,128)}, u32[]{:S(2)}) copy-start(f32[4,8,128]{2,1,0:T(8,128)} %inert.1) | copy-start | bytes 49156
  52.4 9.9 %collective-permute-start.3 = (f32[10,8,128]{2,1,0:T(8,128)S(1)}, f32[10,8,128]{2,1,0:T(8,128)S(1)}, u32[]{:S(2)}, u32[]{:S(2)}) collective-permute-start(f32[10,8,128]{2,1,0:T(8,128)S(1)} %get-tuple-element.54.own), channel_id=1, source_target_pairs={{0,3},{3,0},{1,2},{2,1},{4,7},{7,4},{5,6},{6,5},{8,11},{11,8},{9,1... | collective-permute-start | bytes 122888 | tf_op jit(solution)/shard_map/ppermute | solution.py:516
